TPU v7x, 32 devices: a whole 2x2x4 slice. The times are simulated.
32 devices in a mesh: dp: 2 (over core), row: 4 (over z), col: 4 (over y, x).
Axes of the slice: x: 2, y: 2, z: 4, core: 2. Of those that a mesh axis runs over, the one named last changes fastest.
Arguments:
- tokens: bfloat16 [1024, 8192], P('col', ('dp', 'row')), may hold values from -6.5 to 6.5
- w_qkv: bfloat16 [1024, 3, 1024], P('col', None, 'row'), may hold values from -0.1875 to 0.1875
- b_qv: bfloat16 [2, 1024], P(None, 'row'), may hold values from -0.59765625 to 0.59765625
- w_out: bfloat16 [1024, 1024], P('row', 'col'), may hold values from -1.5 to 1.5
- b_out: bfloat16 [1024], P('col'), may hold values from -2 to 2
- norm1_gain: bfloat16 [1024], P('col'), may hold values from 0.25 to 1.75
- norm1_shift: bfloat16 [1024], P('col'), may hold values from -2 to 2
- w_up: bfloat16 [1024, 4096], P('col', 'row'), may hold values from -0.1875 to 0.1875
- b_up: bfloat16 [4096], P('row'), may hold values from -3 to 3
- w_down: bfloat16 [4096, 1024], P('row', 'col'), may hold values from -0.09375 to 0.09375
- b_down: bfloat16 [1024], P('col'), may hold values from -2 to 2
- norm2_gain: bfloat16 [1024], P('col'), may hold values from 0.25 to 1.75
- norm2_shift: bfloat16 [1024], P('col'), may hold values from -2 to 2
- cotangent: bfloat16 [1024, 8192], P('col', ('dp', 'row')), may hold values from -6 to 6
Outputs:
- out: bfloat16 [1024, 8192], P('col', ('dp', 'row'))
- grad_tokens: float32 [1024, 8192], P('col', ('dp', 'row'))
- grad_w_qkv: float32 [1024, 3, 1024], P('col', None, 'row')
- grad_b_qv: float32 [2, 1024], P(None, 'row')
- grad_w_out: float32 [1024, 1024], P('row', 'col')
- grad_b_out: float32 [1024], P('col')
- grad_norm1_gain: float32 [1024], P('col')
- grad_norm1_shift: float32 [1024], P('col')
- grad_w_up: float32 [1024, 4096], P('col', 'row')
- grad_b_up: float32 [4096], P('row')
- grad_w_down: float32 [4096, 1024], P('row', 'col')
- grad_b_down: float32 [1024], P('col')
- grad_norm2_gain: float32 [1024], P('col')
- grad_norm2_shift: float32 [1024], P('col')
All inputs are finite; a program needn't handle non-finite values.
Results may differ from a plain program's by a relative error of at most 0.014.
Values may be sent and summed in bfloat16 or wider, within the bound.
No kernel may reach another device: no remote copies, remote signals or barrier semaphores. Data moves between devices by JAX's collectives and lax.ppermute only.
A program may use at most 256 MiB of HBM per device.

v0:
```python
import jax
import jax.numpy as jnp
from jax import lax
from jax.sharding import PartitionSpec as P

D = 1024
HEAD_DIM = 64
SEQ = 1024


norm_eps = 1e-05


def matmul(first_mat, second_mat):
    return jnp.dot(first_mat, second_mat, preferred_element_type=jnp.float32)


def against(first_mat, second_mat):
    return lax.dot_general(
        first_mat, second_mat, (((1,), (1,)), ((), ())), preferred_element_type=jnp.float32
    )


def inner_rows(first_mat, second_mat):
    return lax.dot_general(
        first_mat, second_mat, (((0,), (0,)), ((), ())), preferred_element_type=jnp.float32
    )


def by_row(values):
    return lax.all_gather(values, "row", axis=0, tiled=True)


def by_col(values):
    return lax.all_gather(values, "col", axis=0, tiled=True)


def reduce_col(source, weight, transposed):
    row_count = source.shape[0] // lax.axis_size("col")

    def partial_value(row_start, row_num):
        return against(source, weight) if transposed else matmul(source, weight)

    return lax.psum_scatter(
        partial_value(jnp.int32(0), row_count * lax.axis_size("col")),
        "col",
        scatter_dimension=0,
        tiled=True,
    )


def reduce_row(source, weight, transposed):
    row_count = source.shape[0] // lax.axis_size("row")

    def partial_value(row_start, row_num):
        return against(source, weight) if transposed else matmul(source, weight)

    return lax.psum_scatter(
        partial_value(jnp.int32(0), row_count * lax.axis_size("row")),
        "row",
        scatter_dimension=0,
        tiled=True,
    )


def feature_totals(first_terms, second_terms):
    return lax.psum((jnp.sum(first_terms, axis=1), jnp.sum(second_terms, axis=1)), "col")


def norm_forward(residual, gain_vec, shift_vec):
    totals = feature_totals(residual, residual * residual)
    mean_rows = totals[0][:, None] / D
    spread = totals[1][:, None] / D - mean_rows * mean_rows
    scale_rows = lax.rsqrt(spread + norm_eps)
    normed = (residual - mean_rows) * scale_rows
    return (normed * gain_vec + shift_vec, normed, scale_rows)


def norm_backward(grad_in, normed, scale_rows, gain_vec):
    scaled = grad_in * gain_vec
    totals = feature_totals(scaled, scaled * normed)
    grad_resid = scale_rows * (scaled - totals[0][:, None] / D - normed * (totals[1][:, None] / D))
    return (grad_resid, jnp.sum(grad_in * normed, axis=0), jnp.sum(grad_in, axis=0))


def gelu_exact(values):
    return jax.nn.gelu(values, approximate=False)


def by_heads(values, head_count):
    seq_count = values.shape[0] // SEQ
    return values.reshape(seq_count, SEQ, head_count, HEAD_DIM)


def attention_forward(queries, key_seq, value_seq):
    block_len = min(512, SEQ)
    outputs = []
    log_parts = []
    for offset in range(0, SEQ, block_len):
        query_block = queries[:, offset : offset + block_len]
        scores = jnp.einsum(
            "nqhd,nkhd->nhqk", query_block, key_seq, preferred_element_type=jnp.float32
        )
        row_max = jnp.max(scores, axis=-1, keepdims=True)
        exp_scores = jnp.exp(scores - row_max)
        denom = jnp.sum(exp_scores, axis=-1, keepdims=True)
        probs_low = (exp_scores / denom).astype(jnp.bfloat16)
        outputs.append(
            jnp.einsum("nhqk,nkhd->nqhd", probs_low, value_seq, preferred_element_type=jnp.float32)
        )
        log_parts.append(row_max + jnp.log(denom))
    attended = jnp.concatenate(outputs, axis=1)
    rows_here = attended.shape[0] * SEQ
    return (
        attended.reshape(rows_here, -1).astype(jnp.bfloat16),
        jnp.concatenate(log_parts, axis=2),
    )


def attention_backward(queries, key_seq, value_seq, grad_seq, log_norm):
    block_len = min(512, SEQ)
    grad_query_parts = []
    grad_key = jnp.zeros(key_seq.shape, jnp.float32)
    grad_value = jnp.zeros(value_seq.shape, jnp.float32)
    for offset in range(0, SEQ, block_len):
        query_block = queries[:, offset : offset + block_len]
        grad_block = grad_seq[:, offset : offset + block_len]
        scores = jnp.einsum(
            "nqhd,nkhd->nhqk", query_block, key_seq, preferred_element_type=jnp.float32
        )
        probs = jnp.exp(scores - log_norm[:, :, offset : offset + block_len])
        grad_probs = jnp.einsum(
            "nqhd,nkhd->nhqk", grad_block, value_seq, preferred_element_type=jnp.float32
        )
        row_delta = jnp.sum(grad_probs * probs, axis=-1, keepdims=True)
        grad_scores = (probs * (grad_probs - row_delta)).astype(jnp.bfloat16)
        grad_query_parts.append(
            jnp.einsum("nhqk,nkhd->nqhd", grad_scores, key_seq, preferred_element_type=jnp.float32)
        )
        grad_key = grad_key + jnp.einsum(
            "nhqk,nqhd->nkhd", grad_scores, query_block, preferred_element_type=jnp.float32
        )
        grad_value = grad_value + jnp.einsum(
            "nhqk,nqhd->nkhd",
            probs.astype(jnp.bfloat16),
            grad_block,
            preferred_element_type=jnp.float32,
        )
    grad_query = jnp.concatenate(grad_query_parts, axis=1)
    rows_here = grad_query.shape[0] * SEQ
    return (
        grad_query.reshape(rows_here, -1).astype(jnp.bfloat16),
        grad_key.reshape(rows_here, -1).astype(jnp.bfloat16),
        grad_value.reshape(rows_here, -1).astype(jnp.bfloat16),
    )


def shards(
    tokens,
    w_qkv,
    b_qv,
    w_out,
    b_out,
    norm1_gain,
    norm1_shift,
    w_up,
    b_up,
    w_down,
    b_down,
    norm2_gain,
    norm2_shift,
    cotangent,
):
    token_major = tokens.T
    width_col = token_major.shape[1]
    width_row = w_out.shape[0]
    qkv_weight = w_qkv.reshape(width_col, 3 * width_row)
    query_scale = HEAD_DIM ** (-0.5)
    head_count = width_row // HEAD_DIM
    gathered_in = by_row(token_major)
    projected = reduce_col(gathered_in, qkv_weight, False).reshape(-1, 3, width_row)
    queries = ((projected[:, 0] + b_qv[0]) * query_scale).astype(jnp.bfloat16)
    key_rows = projected[:, 1].astype(jnp.bfloat16)
    value_rows = (projected[:, 2] + b_qv[1]).astype(jnp.bfloat16)
    query_seq = by_heads(queries, head_count)
    key_seq = by_heads(key_rows, head_count)
    value_seq = by_heads(value_rows, head_count)
    attended, log_norm = attention_forward(query_seq, key_seq, value_seq)
    gathered_att = by_col(attended)
    attn_out = reduce_row(gathered_att, w_out, False) + b_out
    residual1 = token_major.astype(jnp.float32) + attn_out
    normed_a, normed1, scale1 = norm_forward(residual1, norm1_gain, norm1_shift)
    low_a = normed_a.astype(jnp.bfloat16)
    gathered_a = by_row(low_a)
    pre_act = reduce_col(gathered_a, w_up, False) + b_up
    hidden, gelu_pull = jax.vjp(gelu_exact, pre_act)
    hidden_low = hidden.astype(jnp.bfloat16)
    gathered_h = by_col(hidden_low)
    branch_out = reduce_row(gathered_h, w_down, False)
    residual2 = normed_a + branch_out + b_down
    result, normed2, scale2 = norm_forward(residual2, norm2_gain, norm2_shift)
    grad_out = cotangent.T.astype(jnp.float32)
    grad_r2, gain2_part, shift2_part = norm_backward(grad_out, normed2, scale2, norm2_gain)
    down_bias_part = jnp.sum(grad_r2, axis=0)
    grad_branch = grad_r2.astype(jnp.bfloat16)
    gathered_df = by_row(grad_branch)
    down_grad = inner_rows(gathered_h, gathered_df)
    grad_hidden = reduce_col(gathered_df, w_down, True)
    grad_pre = gelu_pull(grad_hidden)[0].astype(jnp.bfloat16)
    gathered_dz = by_col(grad_pre)
    up_grad = inner_rows(gathered_a, gathered_dz)
    up_bias_grad = jnp.sum(gathered_dz, axis=0, dtype=jnp.float32)
    grad_a_ff = reduce_row(gathered_dz, w_up, True)
    grad_a = grad_r2 + grad_a_ff
    grad_r1, gain1_part, shift1_part = norm_backward(grad_a, normed1, scale1, norm1_gain)
    out_bias_part = jnp.sum(grad_r1, axis=0)
    gathered_datt = by_row(grad_r1.astype(jnp.bfloat16))
    out_grad = inner_rows(gathered_att, gathered_datt)
    grad_attended = reduce_col(gathered_datt, w_out, True).astype(jnp.bfloat16)
    grad_seq = by_heads(grad_attended, head_count)
    grad_query, grad_key, grad_value = attention_backward(
        query_seq, key_seq, value_seq, grad_seq, log_norm
    )
    grad_proj = jnp.stack([grad_query * query_scale, grad_key, grad_value], axis=1).reshape(
        -1, 3 * width_row
    )
    gathered_dqkv = by_col(grad_proj)
    qkv_grad = inner_rows(gathered_in, gathered_dqkv).reshape(width_col, 3, width_row)
    bias_rows = jnp.sum(gathered_dqkv, axis=0, dtype=jnp.float32).reshape(3, width_row)
    qv_bias_grad = jnp.stack([bias_rows[0], bias_rows[2]])
    grad_input = reduce_row(gathered_dqkv, qkv_weight, True) + grad_r1
    norm_sums = lax.psum(
        (gain1_part, shift1_part, gain2_part, shift2_part, out_bias_part, down_bias_part),
        ("dp", "row"),
    )
    weight_sums = lax.psum(
        (qkv_grad, qv_bias_grad, out_grad, up_grad, up_bias_grad, down_grad), "dp"
    )
    return (
        result.astype(jnp.bfloat16).T,
        grad_input.T,
        weight_sums[0],
        weight_sums[1],
        weight_sums[2],
        norm_sums[4],
        norm_sums[0],
        norm_sums[1],
        weight_sums[3],
        weight_sums[4],
        weight_sums[5],
        norm_sums[5],
        norm_sums[2],
        norm_sums[3],
    )


def solution(mesh):
    placed = (
        P("col", ("dp", "row")),
        P("col", None, "row"),
        P(None, "row"),
        P("row", "col"),
        P("col"),
        P("col"),
        P("col"),
        P("col", "row"),
        P("row"),
        P("row", "col"),
        P("col"),
        P("col"),
        P("col"),
        P("col", ("dp", "row")),
    )
    return jax.shard_map(
        shards,
        mesh=mesh,
        in_specs=placed,
        out_specs=(
            P("col", ("dp", "row")),
            P("col", ("dp", "row")),
            P("col", None, "row"),
            P(None, "row"),
            P("row", "col"),
            P("col"),
            P("col"),
            P("col"),
            P("col", "row"),
            P("row"),
            P("row", "col"),
            P("col"),
            P("col"),
            P("col"),
        ),
        check_vma=False,
    )
```

profile of v0, /device:TPU:1, one launch (start us, length us, event | category | flops | bytes accessed | tf_op | source)
XLA Modules:
  0.0 1490.5 jit_solution(4046416394796618080)
XLA Ops:
  10.6 47.7 %all-gather.9.cloned.1.call-done = bf16[4096,256]{1,0:T(8,128)(2,1)} async-done(((bf16[1024,256]{1,0:T(8,128)(2,1)}), bf16[4096,256]{1,0:T(8,128)(2,1)}) %all-gather.9.cloned.1.call-update) | async-done | bytes 2097168 | tf_op jit(solution)/shard_map/all_gather | solution.py:31
  58.2 8.0 fusion.57
  67.1 118.8 %reduce-scatter.9.cloned.1.call-done = f32[1024,768]{1,0:T(8,128)} async-done(((f32[4096,768]{1,0:T(8,128)}), f32[1024,768]{1,0:T(8,128)}) %reduce-scatter.9.cloned.1.call-update) | async-done | bytes 3145744 | tf_op jit(solution)/shard_map/reduce_scatter | solution.py:44
  185.8 3.5 copy.40
  204.5 35.4 %all-gather.11.cloned.1.call-done = bf16[4096,256]{0,1:T(8,128)(2,1)} async-done(((bf16[1024,256]{0,1:T(8,128)(2,1)}), bf16[4096,256]{0,1:T(8,128)(2,1)}) %all-gather.11.cloned.1.call-update) | async-done | bytes 2097168 | tf_op jit(solution)/shard_map/all_gather | solution.py:35
  239.9 4.3 fusion.58
  246.6 74.6 %reduce-scatter.11.cloned.1.call-done = f32[1024,256]{1,0:T(8,128)} async-done(((f32[4096,256]{1,0:T(8,128)}), f32[1024,256]{1,0:T(8,128)}) %reduce-scatter.11.cloned.1.call-update) | async-done | bytes 1048592 | tf_op jit(solution)/shard_map/reduce_scatter | solution.py:58
  322.8 8.0 all-reduce.4
  333.2 46.2 %all-gather.13.cloned.1.call-done = bf16[4096,256]{1,0:T(8,128)(2,1)} async-done(((bf16[1024,256]{1,0:T(8,128)(2,1)}), bf16[4096,256]{1,0:T(8,128)(2,1)}) %all-gather.13.cloned.1.call-update) | async-done | bytes 2097168 | tf_op jit(solution)/shard_map/all_gather | solution.py:31
  379.4 9.7 fusion.59
  389.8 152.0 %reduce-scatter.13.cloned.1.call-done = f32[1024,1024]{1,0:T(8,128)} async-done(((f32[4096,1024]{1,0:T(8,128)}), f32[1024,1024]{1,0:T(8,128)}) %reduce-scatter.13.cloned.1.call-update) | async-done | bytes 4194320 | tf_op jit(solution)/shard_map/reduce_scatter | solution.py:44
  541.8 11.7 multiply_convert_fusion.2
  553.5 87.7 %all-gather.15.cloned.1.call-done = bf16[4096,1024]{1,0:T(8,128)(2,1)} async-done(((bf16[1024,1024]{1,0:T(8,128)(2,1)}), bf16[4096,1024]{1,0:T(8,128)(2,1)}) %all-gather.15.cloned.1.call-update) | async-done | bytes 8388624 | tf_op jit(solution)/shard_map/all_gather | solution.py:35
  641.3 7.7 fusion.60
  652.3 73.6 %reduce-scatter.15.cloned.1.call-done = f32[1024,256]{1,0:T(8,128)} async-done(((f32[4096,256]{1,0:T(8,128)}), f32[1024,256]{1,0:T(8,128)}) %reduce-scatter.15.cloned.1.call-update) | async-done | bytes 1048592 | tf_op jit(solution)/shard_map/reduce_scatter | solution.py:58
  725.9 2.5 fusion.47
  728.4 8.7 all-reduce.3
  738.4 2.3 fusion.39
  740.6 6.9 all-reduce.2
  748.3 3.3 fusion.49
  753.7 49.4 %all-gather.17.cloned.1.call-done = bf16[4096,256]{1,0:T(8,128)(2,1)} async-done(((bf16[1024,256]{1,0:T(8,128)(2,1)}), bf16[4096,256]{1,0:T(8,128)(2,1)}) %all-gather.17.cloned.1.call-update) | async-done | bytes 2097168 | tf_op jit(solution)/shard_map/all_gather | solution.py:31
  803.1 9.7 fusion.61
  812.8 152.6 %reduce-scatter.17.cloned.1.call-done = f32[1024,1024]{1,0:T(8,128)} async-done(((f32[4096,1024]{1,0:T(8,128)}), f32[1024,1024]{1,0:T(8,128)}) %reduce-scatter.17.cloned.1.call-update) | async-done | bytes 4194320 | tf_op jit(solution)/shard_map/reduce_scatter | solution.py:44
  965.5 6.6 add_convert_fusion
  972.2 87.7 %all-gather.19.cloned.1.call-done = bf16[4096,1024]{1,0:T(8,128)(2,1)} async-done(((bf16[1024,1024]{1,0:T(8,128)(2,1)}), bf16[4096,1024]{1,0:T(8,128)(2,1)}) %all-gather.19.cloned.1.call-update) | async-done | bytes 8388624 | tf_op jit(solution)/shard_map/all_gather | solution.py:35
  1059.9 7.7 fusion.62
  1067.8 76.9 %reduce-scatter.19.cloned.1.call-done = f32[1024,256]{1,0:T(8,128)} async-done(((f32[4096,256]{1,0:T(8,128)}), f32[1024,256]{1,0:T(8,128)}) %reduce-scatter.19.cloned.1.call-update) | async-done | bytes 1048592 | tf_op jit(solution)/shard_map/reduce_scatter | solution.py:58
  1144.7 3.1 multiply_reduce_fusion.2
  1147.8 8.0 all-reduce.1
  1155.8 2.4 fusion.51
  1160.1 46.7 %all-gather.21.cloned.1.call-done = bf16[4096,256]{1,0:T(8,128)(2,1)} async-done(((bf16[1024,256]{1,0:T(8,128)(2,1)}), bf16[4096,256]{1,0:T(8,128)(2,1)}) %all-gather.21.cloned.1.call-update) | async-done | bytes 2097168 | tf_op jit(solution)/shard_map/all_gather | solution.py:31
  1206.8 4.3 fusion.63
  1211.8 50.9 %reduce-scatter.21.cloned.1.call-done = f32[1024,256]{1,0:T(8,128)} async-done(((f32[4096,256]{1,0:T(8,128)}), f32[1024,256]{1,0:T(8,128)}) %reduce-scatter.21.cloned.1.call-update) | async-done | bytes 1048592 | tf_op jit(solution)/shard_map/reduce_scatter | solution.py:44
  1264.2 5.0 fusion.5
  1269.2 4.8 multiply_reduce_fusion
  1274.1 4.3 multiply_reduce_fusion.1
  1278.4 4.4 multiply_convert_fusion.1
  1293.4 70.3 %all-gather.23.cloned.1.call-done = bf16[4096,768]{0,1:T(8,128)(2,1)} async-done(((bf16[1024,768]{0,1:T(8,128)(2,1)}), bf16[4096,768]{0,1:T(8,128)(2,1)}) %all-gather.23.cloned.1.call-update) | async-done | bytes 6291472 | tf_op jit(solution)/shard_map/all_gather | solution.py:35
  1363.6 6.6 fusion.64
  1370.6 7.5 fusion.68
  1378.1 6.9 fusion.67
  1390.8 4.7 convert_reduce_fusion
  1395.5 20.2 %all-reduce = (f32[256]{0:T(256)}, f32[256]{0:T(256)}, f32[256]{0:T(256)}, f32[256]{0:T(256)}, f32[256]{0:T(256)}, /*index=5*/f32[256]{0:T(256)}) all-reduce(f32[256]{0:T(256)S(1)} %copy-done.40, f32[256]{0:T(256)S(1)} %copy-done.38, f32[256]{0:T(256)S(1)} %copy-done.39, ...), channel_id=1, replica_groups=mesh['dp'=2,'row'=4,'col'=4] {'dp','row'}, use_global_device_ids=true, to_apply=%region_35.0 | all-reduce | flops 1536 | bytes 12288 | tf_op jit(solution)/shard_map/psum | solution.py:232
  1415.7 3.7 convert_reduce_fusion.1
  1419.5 3.1 all-reduce.5
  1422.6 25.9 %reduce-scatter.23.cloned.1.call-done = f32[1024,256]{1,0:T(8,128)} async-done(((f32[4096,256]{1,0:T(8,128)}), f32[1024,256]{1,0:T(8,128)}) %reduce-scatter.23.cloned.1.call-update) | async-done | bytes 1048592 | tf_op jit(solution)/shard_map/reduce_scatter | solution.py:58
  1451.2 25.2 %all-reduce.9.cloned.1.call-done = (f32[256,3,256]{2,0,1:T(8,128)}, f32[256,256]{1,0:T(8,128)}, f32[256,1024]{1,0:T(8,128)}, f32[1024,256]{1,0:T(8,128)}) async-done(((f32[256,3,256]{2,0,1:T(8,128)}, f32[256,256]{1,0:T(8,128)}, f32[256,1024]{1,0:T(8,128)}, f32[1024,256]{1,0:T(8,128)}), (f32[256,3,256]{2,0,1:T(8,128)}, f32[256,256]{1,0:T(8,128)}, f32[256,1024]{1,0:T(8,128)}, ...) | async-done | bytes 3145744 | tf_op jit(solution)/shard_map/psum | solution.py:236
  1480.3 2.3 copy.52
  (204 shorter events, 62.0 us)
Async XLA Ops:
  7.2 634.1 %copy-start = (bf16[1024,256]{1,0:T(8,128)(2,1)S(1)}, bf16[1024,256]{1,0:T(8,128)(2,1)}, u32[]{:S(2)}) copy-start(bf16[1024,256]{1,0:T(8,128)(2,1)} %param.23) | copy-start | bytes 1572868
  7.2 51.0 %all-gather.9.cloned.1.call-start = ((), (), s32[]{:S(2)}) async-start(), calls=%async_computation.8 | async-start | bytes 2621440 | tf_op jit(solution)/shard_map/all_gather | solution.py:31
  9.4 176.5 %reduce-scatter.9.cloned.1.call-start = ((), (), s32[]{:S(2)}) async-start(), calls=%async_computation.9 | async-start | bytes 15728640 | tf_op jit(solution)/shard_map/reduce_scatter | solution.py:44
  66.2 173.7 %all-gather.11.cloned.1.call-start = ((), (), s32[]{:S(2)}) async-start(), calls=%async_computation.10 | async-start | bytes 2621440 | tf_op jit(solution)/shard_map/all_gather | solution.py:35
  193.9 3.4 copy-start.2
  195.3 6.0 copy-start.3
  195.3 6.0 copy-start.25
  195.5 5.9 copy-start.14
  201.4 38.5 %copy-start.20 = (bf16[256,256]{1,0:T(8,128)(2,1)S(1)}, bf16[256,256]{1,0:T(8,128)(2,1)}, u32[]{:S(2)}) copy-start(bf16[256,256]{1,0:T(8,128)(2,1)} %param.17) | copy-start | bytes 393220
  204.5 116.8 %reduce-scatter.11.cloned.1.call-start = ((), (), s32[]{:S(2)}) async-start(), calls=%async_computation.11 | async-start | bytes 5242880 | tf_op jit(solution)/shard_map/reduce_scatter | solution.py:58
  244.2 77.0 %copy-start.16 = (bf16[256,1024]{0,1:T(8,128)(2,1)S(1)}, bf16[256,1024]{0,1:T(8,128)(2,1)}, u32[]{:S(2)}) copy-start(bf16[256,1024]{0,1:T(8,128)(2,1)} %copy.38) | copy-start | bytes 1572868
  244.2 135.2 %copy-start.22 = (bf16[256,1024]{1,0:T(8,128)(2,1)S(1)}, bf16[256,1024]{1,0:T(8,128)(2,1)}, u32[]{:S(2)}) copy-start(bf16[256,1024]{1,0:T(8,128)(2,1)} %param.21) | copy-start | bytes 1572868
  244.3 135.1 %all-gather.13.cloned.1.call-start = ((), (), s32[]{:S(2)}) async-start(), calls=%async_computation.12 | async-start | bytes 2621440 | tf_op jit(solution)/shard_map/all_gather | solution.py:31
  332.7 209.1 %reduce-scatter.13.cloned.1.call-start = ((), (), s32[]{:S(2)}) async-start(), calls=%async_computation.13 | async-start | bytes 20971520 | tf_op jit(solution)/shard_map/reduce_scatter | solution.py:44
  389.1 252.2 %all-gather.15.cloned.1.call-start = ((), (), s32[]{:S(2)}) async-start(), calls=%async_computation.14 | async-start | bytes 10485760 | tf_op jit(solution)/shard_map/all_gather | solution.py:35
  389.8 163.7 %copy-start.29 = (f32[1024]{0:T(1024)}, f32[1024]{0:T(1024)S(1)}, u32[]{:S(2)}) copy-start(f32[1024]{0:T(1024)S(1)} %convert_element_type.176) | copy-start | bytes 12292
  553.5 172.5 %reduce-scatter.15.cloned.1.call-start = ((), (), s32[]{:S(2)}) async-start(), calls=%async_computation.15 | async-start | bytes 5242880 | tf_op jit(solution)/shard_map/reduce_scatter | solution.py:58
  649.0 154.1 %all-gather.17.cloned.1.call-start = ((), (), s32[]{:S(2)}) async-start(), calls=%async_computation.16 | async-start | bytes 2621440 | tf_op jit(solution)/shard_map/all_gather | solution.py:31
  737.8 2.9 copy-start.28
  753.4 212.0 %reduce-scatter.17.cloned.1.call-start = ((), (), s32[]{:S(2)}) async-start(), calls=%async_computation.17 | async-start | bytes 20971520 | tf_op jit(solution)/shard_map/reduce_scatter | solution.py:44
  812.8 152.7 %copy-start.30 = (f32[1024]{0:T(1024)S(1)}, f32[1024]{0:T(1024)}, u32[]{:S(2)}) copy-start(f32[1024]{0:T(1024)} %copy-done.29) | copy-start | bytes 12292
  812.8 247.1 %all-gather.19.cloned.1.call-start = ((), (), s32[]{:S(2)}) async-start(), calls=%async_computation.18 | async-start | bytes 10485760 | tf_op jit(solution)/shard_map/all_gather | solution.py:35
  965.5 94.5 %copy-start.23 = (bf16[256,1024]{1,0:T(8,128)(2,1)S(1)}, bf16[256,1024]{1,0:T(8,128)(2,1)}, u32[]{:S(2)}) copy-start(bf16[256,1024]{1,0:T(8,128)(2,1)} %param.21) | copy-start | bytes 1572868
  972.1 172.5 %reduce-scatter.19.cloned.1.call-start = ((), (), s32[]{:S(2)}) async-start(), calls=%async_computation.19 | async-start | bytes 5242880 | tf_op jit(solution)/shard_map/reduce_scatter | solution.py:58
  1067.7 77.0 %copy-start.10 = (f32[1024,256]{1,0:T(8,128)S(1)}, f32[1024,256]{1,0:T(8,128)}, u32[]{:S(2)}) copy-start(f32[1024,256]{1,0:T(8,128)} %copy-done.9) | copy-start | bytes 3145732
  1067.7 77.0 %copy-start.35 = (f32[256]{0:T(256)S(1)}, f32[256]{0:T(256)}, u32[]{:S(2)}) copy-start(f32[256]{0:T(256)} %convert_element_type.173) | copy-start | bytes 3076
  1067.7 139.1 %copy-start.21 = (bf16[256,256]{1,0:T(8,128)(2,1)S(1)}, bf16[256,256]{1,0:T(8,128)(2,1)}, u32[]{:S(2)}) copy-start(bf16[256,256]{1,0:T(8,128)(2,1)} %param.17) | copy-start | bytes 393220
  1067.7 139.1 %all-gather.21.cloned.1.call-start = ((), (), s32[]{:S(2)}) async-start(), calls=%async_computation.20 | async-start | bytes 2621440 | tf_op jit(solution)/shard_map/all_gather | solution.py:31
  1160.0 102.7 %reduce-scatter.21.cloned.1.call-start = ((), (), s32[]{:S(2)}) async-start(), calls=%async_computation.21 | async-start | bytes 5242880 | tf_op jit(solution)/shard_map/reduce_scatter | solution.py:44
  1211.1 152.5 %all-gather.23.cloned.1.call-start = ((), (), s32[]{:S(2)}) async-start(), calls=%async_computation.22 | async-start | bytes 7864320 | tf_op jit(solution)/shard_map/all_gather | solution.py:35
  1264.2 5.0 copy-start.15
  1264.2 9.9 slice-start.2
  1269.2 4.9 slice-start.3
  1293.3 155.1 %reduce-scatter.23.cloned.1.call-start = ((), (), s32[]{:S(2)}) async-start(), calls=%async_computation.23 | async-start | bytes 5242880 | tf_op jit(solution)/shard_map/reduce_scatter | solution.py:58
  1370.3 7.8 copy-start.5
  1370.3 106.2 %all-reduce.9.cloned.1.call-start = ((), (), s32[]{:S(2)}) async-start(), calls=%async_computation.24 | async-start | bytes 6291456 | tf_op jit(solution)/shard_map/psum | solution.py:236
  1370.6 15.8 %slice-start.4 = ((s8[6291456]{0:T(1024)(128)(4,1)}), s8[4194304]{0:T(1024)(128)(4,1)S(1)}, s32[]{:S(2)}) async-start(s8[6291456]{0:T(1024)(128)(4,1)} %bitcast.139), calls=%async_computation.29 | async-start | bytes 8388608
  1378.1 6.9 copy-start.4
  1378.1 6.9 copy-start.6
  1378.1 8.3 slice-start.5
  1390.8 4.7 copy-start.36
  1390.8 4.7 copy-start.37
  1390.8 4.7 copy-start.38
  1390.8 4.7 copy-start.39
  1390.8 4.8 copy-start.40
  1395.5 53.0 %copy-start.8 = (f32[1024,256]{1,0:T(8,128)S(1)}, f32[1024,256]{1,0:T(8,128)}, u32[]{:S(2)}) copy-start(f32[1024,256]{1,0:T(8,128)} %copy-done.7) | copy-start | bytes 3145732
  1448.5 35.1 %copy-start.1 = (bf16[1024,256]{1,0:T(8,128)(2,1)S(1)}, bf16[1024,256]{1,0:T(8,128)(2,1)}, u32[]{:S(2)}) copy-start(bf16[1024,256]{1,0:T(8,128)(2,1)} %param.23) | copy-start | bytes 1572868
  1476.4 6.1 copy-start.19
  (24 other events, 32.5 us)
Sparse Core Ops, SparseCore 0:
  10.2 48.0 all-gather.8
  66.3 119.4 reduce-scatter.8
  204.6 35.2 all-gather.10
  244.4 76.7 reduce-scatter.10
  332.8 46.5 all-gather.12
  389.2 152.5 reduce-scatter.12
  553.6 87.6 all-gather.14
  649.1 76.7 reduce-scatter.14
  753.6 49.4 all-gather.16
  812.9 152.5 reduce-scatter.16
  972.3 87.6 all-gather.18
  1067.8 76.7 reduce-scatter.18
  1160.1 46.5 all-gather.20
  1211.2 51.4 reduce-scatter.20
  1293.4 70.1 all-gather.22
  1370.4 78.0 reduce-scatter.22
  1452.2 24.2 all-reduce.8
where the time goes:
time: 1500 us; the launch traced here: 1490 us
  waiting for transfers between devices  1220 us (81%)
  matrix products  103 us (7%)
  other arithmetic  65.5 us (4%)
  blocking collectives  54.9 us (4%)
  local copies, waits for them, and re-layouts  28.5 us (2%)
  between operations  15 us (1%)
    reduce_scatter x4, waiting for transfers between devices, reduce_col(): lax.psum_scatter(partial_value(jnp.int32(0), row_count * lax.axis_size('c...  474 us
    all_gather x4, waiting for transfers between devices, by_col(): return lax.all_gather(values, 'col', axis=0, tiled=True)  281 us
    reduce_scatter x4, waiting for transfers between devices, reduce_row(): lax.psum_scatter(partial_value(jnp.int32(0), row_count * lax.axis_size('r...  251 us
    all_gather x4, waiting for transfers between devices, by_row(): return lax.all_gather(values, 'row', axis=0, tiled=True)  190 us
    psum x4, blocking collectives, feature_totals(): lax.psum((jnp.sum(first_terms, axis=1), jnp.sum(second_terms, axis=1)), '...  31.5 us
  transfers between devices with their start and end apart: 17, of which 17 were waited for; matrix products, arithmetic and copies ran while one was open for 2% of the time, Pallas kernels for 0%

commit v1 on v0

--- a/solution.py
+++ b/solution.py
@@ -1,6 +1,9 @@
 import jax
 import jax.numpy as jnp
 from jax import lax
+from jax.experimental import pallas as pl
+from jax.experimental.pallas import tpu as pltpu
+from jax.sharding import Mesh
 from jax.sharding import PartitionSpec as P
 
 D = 1024
@@ -254,42 +257,429 @@
     )
 
 
+BF = jnp.bfloat16
+F32 = jnp.float32
+PAIR = ((0, 1), (1, 0))
+VMEM_BYTES = 48 * 1024 * 1024
+
+
+def flip(values, axis_name):
+    return lax.ppermute(values, axis_name, PAIR)
+
+
+def shift(values, axis_name, step):
+    size = lax.axis_size(axis_name)
+    return lax.ppermute(values, axis_name, [(i, (i + step) % size) for i in range(size)])
+
+
+def in_order(index, mine, other, axis):
+    first = jnp.where(index == 0, mine, other)
+    second = jnp.where(index == 0, other, mine)
+    return jnp.concatenate([first, second], axis)
+
+
+def four_in_order(low_bit, high_bit, parts, axis):
+    low = [jnp.where(low_bit == 0, parts[i], parts[i ^ 1]) for i in range(4)]
+    full = [jnp.where(high_bit == 0, low[i], low[i ^ 2]) for i in range(4)]
+    return jnp.concatenate(full, axis)
+
+
+def cut(values, index, size, axis):
+    return lax.dynamic_slice_in_dim(values, index * size, size, axis)
+
+
+def attend_kernel(qkv_ref, out_ref, norm_ref):
+    key_t = qkv_ref[0, 1].T
+    value = qkv_ref[0, 2]
+    step = 256
+    for start in range(0, SEQ, step):
+        here = slice(start, start + step)
+        scores = matmul(key_t, qkv_ref[0, 0, :, here])
+        top = jnp.max(scores, axis=0, keepdims=True)
+        weights = jnp.exp(scores - top)
+        denom = jnp.sum(weights, axis=0, keepdims=True)
+        low = (weights * (1.0 / denom)).astype(BF)
+        out_ref[0, :, here] = matmul(value, low).astype(BF)
+        norm_ref[0, :, here] = top + jnp.log(denom)
+
+
+def attend(qkv):
+    heads = qkv.shape[0]
+    return pl.pallas_call(
+        attend_kernel,
+        grid=(heads,),
+        in_specs=[pl.BlockSpec((1, 3, HEAD_DIM, SEQ), lambda h: (h, 0, 0, 0))],
+        out_specs=[
+            pl.BlockSpec((1, HEAD_DIM, SEQ), lambda h: (h, 0, 0)),
+            pl.BlockSpec((1, 1, SEQ), lambda h: (h, 0, 0)),
+        ],
+        out_shape=[
+            jax.ShapeDtypeStruct((heads, HEAD_DIM, SEQ), BF),
+            jax.ShapeDtypeStruct((heads, 1, SEQ), F32),
+        ],
+        compiler_params=pltpu.CompilerParams(vmem_limit_bytes=VMEM_BYTES),
+        name="attend",
+    )(qkv)
+
+
+def attend_back_kernel(qkv_ref, grad_ref, norm_ref, out_ref):
+    key = qkv_ref[0, 1]
+    key_t = key.T
+    value_t = qkv_ref[0, 2].T
+    step = 256
+    grad_key = jnp.zeros((SEQ, HEAD_DIM), F32)
+    grad_value = jnp.zeros((SEQ, HEAD_DIM), F32)
+    for start in range(0, SEQ, step):
+        here = slice(start, start + step)
+        query = qkv_ref[0, 0, :, here]
+        grad = grad_ref[0, :, here]
+        probs = jnp.exp(matmul(key_t, query) - norm_ref[0, :, here])
+        grad_probs = matmul(value_t, grad)
+        delta = jnp.sum(grad_probs * probs, axis=0, keepdims=True)
+        grad_scores = (probs * (grad_probs - delta)).astype(BF)
+        grad_query = matmul(key, grad_scores).astype(BF)
+        out_ref[0, 0, :, here] = (grad_query.astype(F32) * HEAD_DIM**-0.5).astype(BF)
+        grad_key = grad_key + matmul(grad_scores, query.T)
+        grad_value = grad_value + matmul(probs.astype(BF), grad.T)
+    out_ref[0, 1] = grad_key.T.astype(BF)
+    out_ref[0, 2] = grad_value.T.astype(BF)
+
+
+def attend_back(qkv, grad, log_norm):
+    heads = qkv.shape[0]
+    return pl.pallas_call(
+        attend_back_kernel,
+        grid=(heads,),
+        in_specs=[
+            pl.BlockSpec((1, 3, HEAD_DIM, SEQ), lambda h: (h, 0, 0, 0)),
+            pl.BlockSpec((1, HEAD_DIM, SEQ), lambda h: (h, 0, 0)),
+            pl.BlockSpec((1, 1, SEQ), lambda h: (h, 0, 0)),
+        ],
+        out_specs=pl.BlockSpec((1, 3, HEAD_DIM, SEQ), lambda h: (h, 0, 0, 0)),
+        out_shape=jax.ShapeDtypeStruct(qkv.shape, BF),
+        compiler_params=pltpu.CompilerParams(vmem_limit_bytes=VMEM_BYTES),
+        name="attend_back",
+    )(qkv, grad, log_norm)
+
+
+def norm_rows(residual, gain_vec, shift_vec):
+    mean_rows = jnp.mean(residual, axis=1, keepdims=True)
+    spread = jnp.mean(residual * residual, axis=1, keepdims=True) - mean_rows * mean_rows
+    scale_rows = lax.rsqrt(spread + norm_eps)
+    normed = (residual - mean_rows) * scale_rows
+    return normed * gain_vec + shift_vec, normed, scale_rows
+
+
+def norm_rows_back(grad_in, normed, scale_rows, gain_vec):
+    scaled = grad_in * gain_vec
+    first = jnp.mean(scaled, axis=1, keepdims=True)
+    second = jnp.mean(scaled * normed, axis=1, keepdims=True)
+    grad_resid = scale_rows * (scaled - first - normed * second)
+    return grad_resid, jnp.sum(grad_in * normed, axis=0), jnp.sum(grad_in, axis=0)
+
+
+def gather_pair(own):
+    far = flip(own, "t")
+    near = flip(own, "dp")
+    return jnp.concatenate([own, near]), jnp.concatenate([far, flip(far, "dp")])
+
+
+def sum_pair(near_part, far_part, rows):
+    far_sum = far_part[:rows].astype(F32) + flip(far_part[rows:].astype(BF), "dp").astype(F32)
+    sent = flip(far_sum.astype(BF), "t")
+    return near_part[:rows] + flip(near_part[rows:].astype(BF), "dp").astype(F32) + sent.astype(F32)
+
+
+def gather_rows(payload):
+    size = lax.axis_size("row")
+    return jnp.stack([payload] + [shift(payload, "row", step) for step in range(1, size)])
+
+
+def reduce_weights(grads, u_index):
+    size, _, width = grads.shape
+    half = width // 2
+    sent = flip(cut(grads, 1 - u_index, half, 2).astype(BF), "u")
+    both = cut(grads, u_index, half, 2).astype(F32) + sent.astype(F32)
+    total = both[0]
+    for step in range(1, size):
+        total = total + shift(both[step].astype(BF), "row", -step).astype(F32)
+    return total
+
+
+def spread_weights(total, t_index, core):
+    half = total.shape[1] // 2
+    mine = cut(total, t_index, half, 1)
+    other = flip(cut(total, 1 - t_index, half, 1).astype(BF), "t")
+    near = jnp.stack([mine.astype(BF), other])
+    far = flip(near, "dp")
+    return [mine, far[0].astype(F32), other.astype(F32), far[1].astype(F32)]
+
+
+def fast_shards(
+    tokens,
+    w_qkv,
+    b_qv,
+    w_out,
+    b_out,
+    norm1_gain,
+    norm1_shift,
+    w_up,
+    b_up,
+    w_down,
+    b_down,
+    norm2_gain,
+    norm2_shift,
+    cotangent,
+):
+    core, chip = lax.axis_index("dp"), lax.axis_index("t")
+    u_index, row = lax.axis_index("u"), lax.axis_index("row")
+    rows = lax.axis_size("row")
+    quarter = 2 * chip + core
+    other_quarter = 2 * (1 - chip) + core
+    feats = tokens.shape[0]
+    own_rows = SEQ // 4
+    swap_cores = [(2 * d + u, 2 * u + d) for d in range(2) for u in range(2)]
+    scale = HEAD_DIM**-0.5
+
+    tokens_here = lax.ppermute(tokens, ("dp", "u"), swap_cores)
+    tokens_far = flip(tokens_here, "t")
+    tokens_near = flip(tokens_here, "dp")
+    tokens_both = flip(tokens_far, "dp")
+    x_t = four_in_order(chip, core, [tokens_here, tokens_far, tokens_near, tokens_both], 0)
+
+    qkv_local = w_qkv.transpose(1, 2, 0).reshape(3, 4, -1, feats)
+    out_local = w_out.reshape(4, -1, feats)
+    up_local = w_up.T.reshape(4, -1, feats)
+    down_local = w_down.reshape(4, -1, feats)
+    head_rows = qkv_local.shape[2]
+    qkv_rows, out_rows, ff_rows = 3 * head_rows, out_local.shape[1], up_local.shape[1]
+
+    def pick_qkv(index):
+        return lax.dynamic_index_in_dim(qkv_local, index, 1, False).reshape(qkv_rows, feats)
+
+    def pick(array, index):
+        return lax.dynamic_index_in_dim(array, index, 0, False)
+
+    vectors = jnp.stack([b_out, norm1_gain, norm1_shift, b_down, norm2_gain, norm2_shift])
+    vectors = jnp.pad(vectors, ((0, 2), (0, 0)))
+    attn_keep = jnp.concatenate([pick_qkv(quarter), vectors, pick(out_local, quarter)])
+    attn_send = jnp.concatenate([pick_qkv(other_quarter), vectors, pick(out_local, other_quarter)])
+    attn_both = in_order(chip, attn_keep, flip(attn_send, "t"), 1)
+    ff_keep = jnp.concatenate([pick(up_local, quarter), pick(down_local, quarter)])
+    ff_send = jnp.concatenate([pick(up_local, other_quarter), pick(down_local, other_quarter)])
+    ff_both = in_order(chip, ff_keep, flip(ff_send, "t"), 1)
+    width = attn_both.shape[1]
+
+    qv_own = pick(b_qv.reshape(2, 4, -1).transpose(1, 0, 2), quarter).reshape(-1)
+    up_own = pick(b_up.reshape(4, -1), quarter)
+    biases = jnp.pad(jnp.concatenate([qv_own, up_own]), (0, width - qv_own.size - up_own.size))
+    biases = jnp.pad(biases[None], ((0, 7), (0, 0)))
+    qkv_gathered = gather_rows(jnp.concatenate([attn_both[:qkv_rows], biases]))
+    vectors_both = attn_both[qkv_rows : qkv_rows + 8]
+    sent = jnp.concatenate([qkv_gathered[:, :qkv_rows].reshape(-1, width), vectors_both])
+    qkv_full = in_order(u_index, sent, flip(sent, "u"), 1)
+    qkv_full, vec = qkv_full[: rows * qkv_rows], qkv_full[rows * qkv_rows :].astype(F32)
+    bias_rows = qkv_gathered[:, qkv_rows].astype(F32)
+    bias_q, bias_v = bias_rows[:, :head_rows], bias_rows[:, head_rows : 2 * head_rows]
+    bias_up = bias_rows[:, 2 * head_rows : 2 * head_rows + ff_rows].reshape(1, -1)
+
+    def gather_weight(payload):
+        gathered = gather_rows(payload).reshape(-1, width)
+        return in_order(u_index, gathered, flip(gathered, "u"), 1)
+
+    out_full = gather_weight(attn_both[qkv_rows + 8 :])
+    up_full = gather_weight(ff_both[:ff_rows])
+    down_full = gather_weight(ff_both[ff_rows:])
+
+    projected = matmul(qkv_full, x_t).reshape(rows, 3, head_rows, SEQ)
+    qkv = jnp.stack(
+        [
+            (projected[:, 0] + bias_q[:, :, None]) * scale,
+            projected[:, 1],
+            projected[:, 2] + bias_v[:, :, None],
+        ],
+        axis=1,
+    ).astype(BF)
+    attended, log_norm = attend(qkv)
+    attended = attended.reshape(rows * head_rows, SEQ)
+    attended = jnp.concatenate([cut(attended, quarter ^ j, own_rows, 1) for j in range(4)], 1)
+    half = SEQ // 2
+    far_out = inner_rows(attended[:, half:], out_full)
+    near_out = inner_rows(attended[:, :half], out_full)
+    attn_out = sum_pair(near_out, far_out, own_rows) + vec[0]
+    residual1 = cut(x_t, quarter, own_rows, 1).T.astype(F32) + attn_out
+    normed_a, normed1, scale1 = norm_rows(residual1, vec[1], vec[2])
+
+    near_a, far_a = gather_pair(normed_a.astype(BF))
+
+    def up(rows_in):
+        pre = against(rows_in, up_full) + bias_up
+        cdf = 0.5 * (1.0 + lax.erf(pre * (0.5**0.5)))
+        slope = cdf + pre * (jnp.exp(-0.5 * pre * pre) * 0.3989422804014327)
+        return (pre * cdf).astype(BF), slope
+
+    hidden_near, slope_near = up(near_a)
+    hidden_far, slope_far = up(far_a)
+    far_branch = matmul(hidden_far, down_full)
+    near_branch = matmul(hidden_near, down_full)
+    residual2 = normed_a + sum_pair(near_branch, far_branch, own_rows) + vec[3]
+    result, normed2, scale2 = norm_rows(residual2, vec[4], vec[5])
+
+    cot = lax.ppermute(cotangent, ("dp", "u"), swap_cores)
+    cot_parts = [cut(cot, quarter ^ j, own_rows, 1) for j in range(4)]
+    cot_far = flip(jnp.stack([cot_parts[2], cot_parts[3]]), "t")
+    cot_mine = jnp.stack([cot_parts[0], cot_far[0]])
+    cot_near = flip(jnp.stack([cot_parts[1], cot_far[1]]), "dp")
+    grad_out = four_in_order(chip, core, [cot_mine[0], cot_mine[1], cot_near[0], cot_near[1]], 0)
+    grad_out = grad_out.T.astype(F32)
+    grad_r2, gain2_part, shift2_part = norm_rows_back(grad_out, normed2, scale2, vec[4])
+    down_bias_part = jnp.sum(grad_r2, axis=0)
+
+    near_g, far_g = gather_pair(grad_r2.astype(BF))
+    grad_pre_near = (against(near_g, down_full) * slope_near).astype(BF)
+    grad_pre_far = (against(far_g, down_full) * slope_far).astype(BF)
+    far_back = matmul(grad_pre_far, up_full)
+    near_back = matmul(grad_pre_near, up_full)
+    grad_a = grad_r2 + sum_pair(near_back, far_back, own_rows)
+    grad_r1, gain1_part, shift1_part = norm_rows_back(grad_a, normed1, scale1, vec[1])
+    out_bias_part = jnp.sum(grad_r1, axis=0)
+
+    hidden_all = jnp.concatenate([hidden_near, hidden_far])
+    g_all = jnp.concatenate([near_g, far_g])
+    a_all = jnp.concatenate([near_a, far_a])
+    grad_pre_all = jnp.concatenate([grad_pre_near, grad_pre_far])
+    down_grad = inner_rows(hidden_all, g_all).reshape(rows, ff_rows, -1)
+    up_grad = inner_rows(grad_pre_all, a_all).reshape(rows, ff_rows, -1)
+    up_bias = jnp.sum(grad_pre_all, axis=0, dtype=F32).reshape(rows, 1, ff_rows)
+    up_bias = jnp.tile(up_bias, (1, 1, up_grad.shape[2] // ff_rows))
+    up_grad = jnp.concatenate([up_grad, jnp.pad(up_bias, ((0, 0), (0, 7), (0, 0)))], 1)
+    down_total = reduce_weights(down_grad, u_index)
+    up_total = reduce_weights(up_grad, u_index)
+
+    def in_tokens(values):
+        parts = [values[:, j * own_rows : (j + 1) * own_rows] for j in range(4)]
+        return four_in_order(core, chip, parts, 1)
+
+    near_d, far_d = gather_pair(grad_r1.astype(BF))
+    d_all = jnp.concatenate([near_d, far_d])
+    grad_att = in_tokens(against(out_full, d_all).astype(BF)).reshape(rows, HEAD_DIM, SEQ)
+    out_grad = matmul(attended, d_all).reshape(rows, out_rows, -1)
+    grad_proj = attend_back(qkv, grad_att, log_norm).reshape(rows * qkv_rows, SEQ)
+
+    block = feats
+    own_block, near_block = 2 * core + chip, 2 * (1 - core) + chip
+    far_block, both_block = 2 * core + 1 - chip, 2 * (1 - core) + 1 - chip
+
+    def back_to(index):
+        return inner_rows(cut(qkv_full, index, block, 1), grad_proj)
+
+    far_in = back_to(far_block) + flip(back_to(both_block).astype(BF), "dp").astype(F32)
+    far_in = flip(far_in.astype(BF), "t")
+    near_in = back_to(own_block) + flip(back_to(near_block).astype(BF), "dp").astype(F32)
+    passed = in_tokens(cut(d_all, own_block, block, 1).T)
+    grad_in = near_in + far_in.astype(F32) + passed.astype(F32)
+    grad_tokens = lax.ppermute(grad_in.astype(BF), ("dp", "u"), swap_cores).astype(F32)
+
+    qkv_grad = against(grad_proj, x_t).reshape(rows, qkv_rows, -1)
+    proj_sums = jnp.sum(grad_proj.reshape(rows, 3, head_rows, SEQ), axis=3, dtype=F32)
+    qv_bias = jnp.concatenate([proj_sums[:, 0], proj_sums[:, 2]], 1)[:, None]
+    qv_bias = jnp.tile(qv_bias, (1, 1, qkv_grad.shape[2] // qv_bias.shape[2]))
+    norm_part = jnp.stack(
+        [out_bias_part, gain1_part, shift1_part, down_bias_part, gain2_part, shift2_part]
+    )
+    norm_part = jnp.broadcast_to(norm_part, (rows, *norm_part.shape))
+    extra = jnp.pad(jnp.concatenate([norm_part, qv_bias], 1), ((0, 0), (0, 1), (0, 0)))
+    qkv_total = reduce_weights(jnp.concatenate([qkv_grad, extra], 1), u_index)
+    out_total = reduce_weights(out_grad, u_index)
+
+    ff_parts = spread_weights(jnp.concatenate([down_total, up_total]), chip, core)
+    attn_parts = spread_weights(jnp.concatenate([out_total, qkv_total]), chip, core)
+
+    def quarters(parts, start, stop):
+        picked = [part[start:stop] for part in parts]
+        return four_in_order(core, chip, [p[None] for p in picked], 0)
+
+    down_out = quarters(ff_parts, 0, ff_rows).reshape(4 * ff_rows, -1)
+    up_out = quarters(ff_parts, ff_rows, 2 * ff_rows).reshape(4 * ff_rows, -1).T
+    up_bias_out = quarters(ff_parts, 2 * ff_rows, 2 * ff_rows + 1)[:, 0, :ff_rows].reshape(-1)
+    out_out = quarters(attn_parts, 0, out_rows).reshape(4 * out_rows, -1)
+    qkv_out = quarters(attn_parts, out_rows, out_rows + qkv_rows)
+    qkv_out = qkv_out.reshape(4, 3, head_rows, -1).transpose(3, 1, 0, 2).reshape(feats, 3, -1)
+    first_extra = out_rows + qkv_rows
+    norm_out = sum(part[first_extra : first_extra + 6] for part in attn_parts)
+    qv_out = quarters(attn_parts, first_extra + 6, first_extra + 7)[:, 0, : 2 * head_rows]
+    qv_out = qv_out.reshape(4, 2, head_rows).transpose(1, 0, 2).reshape(2, -1)
+
+    result_t = result.astype(BF).T.reshape(2, 2, feats, own_rows)
+    result_here = lax.dynamic_index_in_dim(result_t, chip, 1, False)
+    result_far = flip(lax.dynamic_index_in_dim(result_t, 1 - chip, 1, False), "t")
+    result_pair = jnp.stack([result_here, result_far])
+    result_own = lax.dynamic_index_in_dim(result_pair, core, 1, False)
+    result_near = flip(lax.dynamic_index_in_dim(result_pair, 1 - core, 1, False), "dp")
+    result_parts = [result_own[0], result_near[0], result_own[1], result_near[1]]
+    result_seq = four_in_order(core, chip, result_parts, 1)
+    result_out = lax.ppermute(result_seq, ("dp", "u"), swap_cores)
+    return (
+        result_out,
+        grad_tokens,
+        qkv_out,
+        qv_out,
+        out_out,
+        norm_out[0],
+        norm_out[1],
+        norm_out[2],
+        up_out,
+        up_bias_out,
+        down_out,
+        norm_out[3],
+        norm_out[4],
+        norm_out[5],
+    )
+
+
 def solution(mesh):
-    placed = (
-        P("col", ("dp", "row")),
-        P("col", None, "row"),
-        P(None, "row"),
-        P("row", "col"),
-        P("col"),
-        P("col"),
-        P("col"),
-        P("col", "row"),
-        P("row"),
-        P("row", "col"),
-        P("col"),
-        P("col"),
-        P("col"),
-        P("col", ("dp", "row")),
-    )
+    sizes = dict(mesh.shape)
+    grouped = sizes["dp"] == 2 and sizes["col"] == 4 and D % (4 * sizes["row"] * HEAD_DIM) == 0
+    if grouped:
+        devices = mesh.devices.reshape(sizes["dp"], sizes["row"], 2, 2)
+        inner_mesh, col, body = Mesh(devices, ("dp", "row", "u", "t")), ("u", "t"), fast_shards
+    else:
+        inner_mesh, col, body = mesh, "col", shards
+    tokens_spec = P(col, ("dp", "row"))
     return jax.shard_map(
-        shards,
-        mesh=mesh,
-        in_specs=placed,
+        body,
+        mesh=inner_mesh,
+        in_specs=(
+            tokens_spec,
+            P(col, None, "row"),
+            P(None, "row"),
+            P("row", col),
+            P(col),
+            P(col),
+            P(col),
+            P(col, "row"),
+            P("row"),
+            P("row", col),
+            P(col),
+            P(col),
+            P(col),
+            tokens_spec,
+        ),
         out_specs=(
-            P("col", ("dp", "row")),
-            P("col", ("dp", "row")),
-            P("col", None, "row"),
+            tokens_spec,
+            tokens_spec,
+            P(col, None, "row"),
             P(None, "row"),
-            P("row", "col"),
-            P("col"),
-            P("col"),
-            P("col"),
-            P("col", "row"),
+            P("row", col),
+            P(col),
+            P(col),
+            P(col),
+            P(col, "row"),
             P("row"),
-            P("row", "col"),
-            P("col"),
-            P("col"),
-            P("col"),
+            P("row", col),
+            P(col),
+            P(col),
+            P(col),
         ),
         check_vma=False,
     )

time: 1500 us -> 481 us (0.32)
  the two profiles are of different devices: /device:TPU:1 before, /device:TPU:9 now
where the time goes in v1:
time: 481 us; the launch traced here: 472 us
  waiting for transfers between devices  254 us (53%)
  starting transfers between devices  83.4 us (17%)
  matrix products  39.8 us (8%)
  other arithmetic  36.1 us (8%)
  Pallas kernels  28.8 us (6%)
  local copies, waits for them, and re-layouts  27.7 us (6%)
    ppermute x42, waiting for transfers between devices, flip(): return lax.ppermute(values, axis_name, PAIR)  137 us
    ppermute x24, waiting for transfers between devices, shift(): lax.ppermute(values, axis_name, [(i, (i + step) % size) for i in range(si...  105 us
    ppermute x42, starting transfers between devices, flip(): return lax.ppermute(values, axis_name, PAIR)  42.7 us
    ppermute x24, starting transfers between devices, shift(): lax.ppermute(values, axis_name, [(i, (i + step) % size) for i in range(si...  29.6 us
    dot_general x6, matrix products, against(): lax.dot_general(first_mat, second_mat, (((1,), (1,)), ((), ())), preferre...  15.9 us
    pallas_call x1, Pallas kernels, attend_back(): pl.pallas_call(attend_back_kernel, grid=(heads,), in_specs=[pl.BlockSpec(...  15.6 us
    dot_general x8, matrix products, inner_rows(): lax.dot_general(first_mat, second_mat, (((0,), (0,)), ((), ())), preferre...  15.2 us
    unnamed x129, local copies, waits for them, and re-layouts  13.3 us
  transfers between devices with their start and end apart: 70, of which 35 were waited for; matrix products, arithmetic and copies ran while one was open for 18% of the time, Pallas kernels for 6%

profile of v1, /device:TPU:9, one launch (start us, length us, event | category | flops | bytes accessed | tf_op | source)
XLA Modules:
  0.0 472.2 jit_solution(10042713968683266037)
XLA Ops:
  8.0 4.0 collective-permute-start
  19.8 3.1 collective-permute-done.7
  22.9 3.2 collective-permute-start.10
  26.2 5.4 %collective-permute-done.6 = bf16[200,512]{1,0:T(8,128)(2,1)S(1)} collective-permute-done((bf16[200,512]{1,0:T(8,128)(2,1)S(1)}, bf16[200,512]{1,0:T(8,128)(2,1)S(1)}, u32[]{:S(2)}, u32[]{:S(2)}) %collective-permute-start.6) | collective-permute-done | bytes 204832 | tf_op jit(solution)/shard_map/ppermute | solution.py:272
  31.6 4.5 collective-permute-start.9
  42.5 9.2 %collective-permute-done.1 = bf16[256,1024]{1,0:T(8,128)(2,1)S(1)} collective-permute-done((bf16[256,1024]{1,0:T(8,128)(2,1)S(1)}, bf16[256,1024]{1,0:T(8,128)(2,1)S(1)}, u32[]{:S(2)}, u32[]{:S(2)}) %collective-permute-start.1) | collective-permute-done | bytes 524320 | tf_op jit(solution)/shard_map/ppermute | solution.py:267
  54.1 9.7 %collective-permute-done.12 = bf16[256,512]{1,0:T(8,128)(2,1)S(1)} collective-permute-done((bf16[256,512]{1,0:T(8,128)(2,1)S(1)}, bf16[256,512]{1,0:T(8,128)(2,1)S(1)}, u32[]{:S(2)}, u32[]{:S(2)}) %collective-permute-start.12) | collective-permute-done | bytes 262176 | tf_op jit(solution)/shard_map/ppermute | solution.py:267
  67.9 13.2 %attend.1 = (bf16[4,64,1024]{2,1,0:T(8,128)(2,1)S(1)}, f32[4,1,1024]{2,1,0:T(1,128)S(1)}) custom-call(bf16[4,3,64,1024]{3,2,1,0:T(8,128)(2,1)S(1)} %pad_maximum_fusion.5.qkv_ref), custom_call_target="tpu_custom_call" | custom-call | tf_op jit(solution)/shard_map/attend/pallas_call | solution.py:308
  82.4 3.3 collective-permute-start.19
  87.8 3.4 collective-permute-done.20
  93.0 8.7 %collective-permute-done.19 = bf16[256,512]{1,0:T(8,128)(2,1)S(1)} collective-permute-done((bf16[256,512]{1,0:T(8,128)(2,1)S(1)}, bf16[256,512]{1,0:T(8,128)(2,1)S(1)}, u32[]{:S(2)}, u32[]{:S(2)}) %collective-permute-start.19) | collective-permute-done | bytes 262176 | tf_op jit(solution)/shard_map/ppermute | solution.py:272
  102.6 15.8 %collective-permute-done.18 = bf16[256,512]{1,0:T(8,128)(2,1)S(1)} collective-permute-done((bf16[256,512]{1,0:T(8,128)(2,1)S(1)}, bf16[256,512]{1,0:T(8,128)(2,1)S(1)}, u32[]{:S(2)}, u32[]{:S(2)}) %collective-permute-start.18) | collective-permute-done | bytes 262176 | tf_op jit(solution)/shard_map/ppermute | solution.py:272
  119.2 5.7 %collective-permute-done.24 = bf16[256,512]{1,0:T(8,128)(2,1)S(1)} collective-permute-done((bf16[256,512]{1,0:T(8,128)(2,1)S(1)}, bf16[256,512]{1,0:T(8,128)(2,1)S(1)}, u32[]{:S(2)}, u32[]{:S(2)}) %collective-permute-start.24) | collective-permute-done | bytes 262176 | tf_op jit(solution)/shard_map/ppermute | solution.py:272
  124.9 2.8 collective-permute-start.34
  132.9 8.1 %collective-permute-done.34 = bf16[256,1024]{1,0:T(8,128)(2,1)S(1)} collective-permute-done((bf16[256,1024]{1,0:T(8,128)(2,1)S(1)}, bf16[256,1024]{1,0:T(8,128)(2,1)S(1)}, u32[]{:S(2)}, u32[]{:S(2)}) %collective-permute-start.34) | collective-permute-done | bytes 524320 | tf_op jit(solution)/shard_map/ppermute | solution.py:528
  141.4 2.8 collective-permute-done.27
  144.3 4.2 collective-permute-start.28
  148.4 11.3 %collective-permute-done.21 = bf16[1024,512]{1,0:T(8,128)(2,1)S(1)} collective-permute-done((bf16[1024,512]{1,0:T(8,128)(2,1)S(1)}, bf16[1024,512]{1,0:T(8,128)(2,1)S(1)}, u32[]{:S(2)}, u32[]{:S(2)}) %collective-permute-start.21) | collective-permute-done | bytes 1048608 | tf_op jit(solution)/shard_map/ppermute | solution.py:267
  160.0 4.2 collective-permute-start.16
  164.2 14.4 %collective-permute-done.25 = bf16[1024,512]{1,0:T(8,128)(2,1)S(1)} collective-permute-done((bf16[1024,512]{1,0:T(8,128)(2,1)S(1)}, bf16[1024,512]{1,0:T(8,128)(2,1)S(1)}, u32[]{:S(2)}, u32[]{:S(2)}) %collective-permute-start.25) | collective-permute-done | bytes 1048608 | tf_op jit(solution)/shard_map/ppermute | solution.py:267
  180.2 3.1 multiply_convert_fusion.1
  184.7 2.5 collective-permute-start.29
  191.5 10.6 %collective-permute-done.30 = bf16[256,1024]{0,1:T(8,128)(2,1)S(1)} collective-permute-done((bf16[256,1024]{0,1:T(8,128)(2,1)S(1)}, bf16[256,1024]{0,1:T(8,128)(2,1)S(1)}, u32[]{:S(2)}, u32[]{:S(2)}) %collective-permute-start.30) | collective-permute-done | bytes 524320 | tf_op jit(solution)/shard_map/ppermute | solution.py:267
  209.7 13.1 %collective-permute-done.31 = bf16[2,256,256]{2,1,0:T(8,128)(2,1)} collective-permute-done((bf16[2,256,256]{2,1,0:T(8,128)(2,1)}, bf16[2,256,256]{2,1,0:T(8,128)(2,1)}, u32[]{:S(2)}, u32[]{:S(2)}) %collective-permute-start.31) | collective-permute-done | bytes 262176 | tf_op jit(solution)/shard_map/ppermute | solution.py:267
  226.4 4.9 %fusion.5 = bf16[512,1024]{1,0:T(8,128)(2,1)S(1)} fusion(f32[512,1024]{1,0:T(8,128)} %get-tuple-element.238, bf16[256,1024]{0,1:T(8,128)(2,1)} %collective-permute-done.37, bf16[256,1024]{0,1:T(8,128)(2,1)} %get-tuple-element.147, f32[1024]{0:T(1024)S(1)} %bitcast.595, bf16[1024,512]{1,0:T(8,128)(2,1)} %copy-done.25, bf16[1024,512]{1,0:T(8,128)(2,1)} %copy-done.23), kind=kOutput, calls=%fused_computation.15 | convolution fusion | flops 1085800448 | bytes 6295552 | tf_op jit(solution)/shard_map/dot_general | solution.py:22
  239.3 2.8 fusion.11
  245.7 3.2 collective-permute-start.41
  248.9 4.4 fusion.23
  253.7 2.9 select_maximum_fusion
  259.8 3.9 fusion.12
  264.3 8.8 %collective-permute-done.42 = bf16[256,1024]{0,1:T(8,128)(2,1)S(1)} collective-permute-done((bf16[256,1024]{0,1:T(8,128)(2,1)S(1)}, bf16[256,1024]{0,1:T(8,128)(2,1)S(1)}, u32[]{:S(2)}, u32[]{:S(2)}) %collective-permute-start.42) | collective-permute-done | bytes 524320 | tf_op jit(solution)/shard_map/ppermute | solution.py:267
  276.6 28.2 %collective-permute-done.60 = bf16[4,256,512]{2,1,0:T(8,128)(2,1)S(1)} collective-permute-done((bf16[4,256,512]{2,1,0:T(8,128)(2,1)S(1)}, bf16[4,256,512]{2,1,0:T(8,128)(2,1)S(1)}, u32[]{:S(2)}, u32[]{:S(2)}) %collective-permute-start.60) | collective-permute-done | bytes 1048608 | tf_op jit(solution)/shard_map/ppermute | solution.py:267
  307.7 4.9 %collective-permute-done.63 = bf16[256,512]{1,0:T(8,128)(2,1)S(1)} collective-permute-done((bf16[256,512]{1,0:T(8,128)(2,1)S(1)}, bf16[256,512]{1,0:T(8,128)(2,1)S(1)}, u32[]{:S(2)}, u32[]{:S(2)}) %collective-permute-start.63) | collective-permute-done | bytes 262176 | tf_op jit(solution)/shard_map/ppermute | solution.py:272
  312.8 14.7 %collective-permute-done.62 = bf16[256,512]{1,0:T(8,128)(2,1)S(1)} collective-permute-done((bf16[256,512]{1,0:T(8,128)(2,1)S(1)}, bf16[256,512]{1,0:T(8,128)(2,1)S(1)}, u32[]{:S(2)}, u32[]{:S(2)}) %collective-permute-start.62) | collective-permute-done | bytes 262176 | tf_op jit(solution)/shard_map/ppermute | solution.py:272
  327.5 3.1 collective-permute-start.66
  330.6 10.9 %collective-permute-done.61 = bf16[256,512]{1,0:T(8,128)(2,1)S(1)} collective-permute-done((bf16[256,512]{1,0:T(8,128)(2,1)S(1)}, bf16[256,512]{1,0:T(8,128)(2,1)S(1)}, u32[]{:S(2)}, u32[]{:S(2)}) %collective-permute-start.61) | collective-permute-done | bytes 262176 | tf_op jit(solution)/shard_map/ppermute | solution.py:272
  341.7 3.2 collective-permute-done.67
  347.2 3.5 collective-permute-done.66
  355.5 6.3 %collective-permute-done.68 = bf16[520,256]{1,0:T(8,128)(2,1)} collective-permute-done((bf16[520,256]{1,0:T(8,128)(2,1)}, bf16[520,256]{1,0:T(8,128)(2,1)}, u32[]{:S(2)}, u32[]{:S(2)}) %collective-permute-start.68) | collective-permute-done | bytes 266272 | tf_op jit(solution)/shard_map/ppermute | solution.py:267
  371.6 15.6 %attend_back.1 = bf16[4,3,64,1024]{3,2,1,0:T(8,128)(2,1)S(1)} custom-call(bf16[4,3,64,1024]{3,2,1,0:T(8,128)(2,1)S(1)} %pad_maximum_fusion.5.qkv_ref, bf16[4,64,1024]{2,1,0:T(8,128)(2,1)S(1)} %bitcast.522, f32[4,1,1024]{2,1,0:T(1,128)S(1)} %get-tuple-element.17.norm_ref), custom_call_target="tpu_custom_call" | custom-call | tf_op jit(solution)/shard_map/attend_back/pallas_call | solution.py:350
  390.7 3.0 fusion.31
  399.9 19.4 %collective-permute-done.50 = bf16[4,64,512]{2,1,0:T(8,128)(2,1)S(1)} collective-permute-done((bf16[4,64,512]{2,1,0:T(8,128)(2,1)S(1)}, bf16[4,64,512]{2,1,0:T(8,128)(2,1)S(1)}, u32[]{:S(2)}, u32[]{:S(2)}) %collective-permute-start.50) | collective-permute-done | bytes 262176 | tf_op jit(solution)/shard_map/ppermute | solution.py:267
  419.5 3.3 collective-permute-start.52
  425.9 2.5 collective-permute-done.51
  434.6 11.3 %collective-permute-done.56 = bf16[200,512]{1,0:T(8,128)(2,1)S(1)} collective-permute-done((bf16[200,512]{1,0:T(8,128)(2,1)S(1)}, bf16[200,512]{1,0:T(8,128)(2,1)S(1)}, u32[]{:S(2)}, u32[]{:S(2)}) %collective-permute-start.56) | collective-permute-done | bytes 204832 | tf_op jit(solution)/shard_map/ppermute | solution.py:272
  445.9 3.9 collective-permute-done.55
  451.0 2.5 copy.184
  464.7 4.3 collective-permute-done.49
  (389 shorter events, 131.7 us)
Async XLA Ops:
  8.0 30.7 %collective-permute-start = (bf16[256,1024]{1,0:T(8,128)(2,1)}, bf16[256,1024]{1,0:T(8,128)(2,1)S(1)}, u32[]{:S(2)}, u32[]{:S(2)}) collective-permute-start(bf16[256,1024]{1,0:T(8,128)(2,1)} %param.14), channel_id=1, source_target_pairs={{0,0},{2,16},{16,2},{18,18},{1,1},{3,17},{17,3},{19,19},{4,4},{6,2... | collective-permute-start | bytes 1572872 | tf_op jit(solution)/shard_map/ppermute | solution.py:444
  15.3 16.3 %collective-permute-start.6 = (bf16[200,512]{1,0:T(8,128)(2,1)S(1)}, bf16[200,512]{1,0:T(8,128)(2,1)S(1)}, u32[]{:S(2)}, u32[]{:S(2)}) collective-permute-start(bf16[200,512]{1,0:T(8,128)(2,1)S(1)} %get-tuple-element.219), channel_id=1, source_target_pairs={{0,8},{4,12},{8,0},{12,4},{1,9},{5,13},{9,1},{13,5},{2,10},{6,14},... | collective-permute-start | bytes 614408 | tf_op jit(solution)/shard_map/ppermute | solution.py:272
  17.6 20.8 %collective-permute-start.5 = (bf16[200,512]{1,0:T(8,128)(2,1)S(1)}, bf16[200,512]{1,0:T(8,128)(2,1)S(1)}, u32[]{:S(2)}, u32[]{:S(2)}) collective-permute-start(bf16[200,512]{1,0:T(8,128)(2,1)S(1)} %get-tuple-element.219), channel_id=1, source_target_pairs={{0,4},{4,8},{8,12},{12,0},{1,5},{5,9},{9,13},{13,1},{2,6},{6,10},{... | collective-permute-start | bytes 614408 | tf_op jit(solution)/shard_map/ppermute | solution.py:272
  19.8 19.3 %collective-permute-start.11 = (bf16[64,512]{1,0:T(8,128)(2,1)S(1)}, bf16[64,512]{1,0:T(8,128)(2,1)S(1)}, u32[]{:S(2)}, u32[]{:S(2)}) collective-permute-start(bf16[64,512]{1,0:T(8,128)(2,1)S(1)} %pad_maximum_fusion.32), channel_id=1, source_target_pairs={{0,12},{4,0},{8,4},{12,8},{1,13},{5,1},{9,5},{13,9},{2,14},{6,2},{... | collective-permute-start | bytes 196616 | tf_op jit(solution)/shard_map/ppermute | solution.py:272
  22.9 17.4 %collective-permute-start.10 = (bf16[64,512]{1,0:T(8,128)(2,1)S(1)}, bf16[64,512]{1,0:T(8,128)(2,1)S(1)}, u32[]{:S(2)}, u32[]{:S(2)}) collective-permute-start(bf16[64,512]{1,0:T(8,128)(2,1)S(1)} %pad_maximum_fusion.32), channel_id=1, source_target_pairs={{0,8},{4,12},{8,0},{12,4},{1,9},{5,13},{9,1},{13,5},{2,10},{6,14},... | collective-permute-start | bytes 196616 | tf_op jit(solution)/shard_map/ppermute | solution.py:272
  38.6 25.3 %collective-permute-start.8 = (bf16[776,512]{1,0:T(8,128)(2,1)S(1)}, bf16[776,512]{1,0:T(8,128)(2,1)S(1)}, u32[]{:S(2)}, u32[]{:S(2)}) collective-permute-start(bf16[776,512]{1,0:T(8,128)(2,1)S(1)} %pad_maximum_fusion.12), channel_id=1, source_target_pairs={{0,2},{2,0},{1,3},{3,1},{4,6},{6,4},{5,7},{7,5},{8,10},{10,8},{9,1... | collective-permute-start | bytes 2383880 | tf_op jit(solution)/shard_map/ppermute | solution.py:267
  38.7 13.0 %collective-permute-start.1 = (bf16[256,1024]{1,0:T(8,128)(2,1)S(1)}, bf16[256,1024]{1,0:T(8,128)(2,1)S(1)}, u32[]{:S(2)}, u32[]{:S(2)}) collective-permute-start(bf16[256,1024]{1,0:T(8,128)(2,1)S(1)} %collective-permute-done), channel_id=1, source_target_pairs={{0,1},{1,0},{2,3},{3,2},{4,5},{5,4},{6,7},{7,6},{8,9},{9,8},{10,11... | collective-permute-start | bytes 1572872 | tf_op jit(solution)/shard_map/ppermute | solution.py:267
  39.1 43.1 %collective-permute-start.17 = (bf16[512,256]{1,0:T(8,128)(2,1)S(1)}, bf16[512,256]{1,0:T(8,128)(2,1)S(1)}, u32[]{:S(2)}, u32[]{:S(2)}) collective-permute-start(bf16[512,256]{1,0:T(8,128)(2,1)S(1)} %pad_maximum_fusion.22), channel_id=1, source_target_pairs={{0,1},{1,0},{2,3},{3,2},{4,5},{5,4},{6,7},{7,6},{8,9},{9,8},{10,11... | collective-permute-start | bytes 786440 | tf_op jit(solution)/shard_map/ppermute | solution.py:267
  40.8 23.1 %collective-permute-start.12 = (bf16[256,512]{1,0:T(8,128)(2,1)S(1)}, bf16[256,512]{1,0:T(8,128)(2,1)S(1)}, u32[]{:S(2)}, u32[]{:S(2)}) collective-permute-start(bf16[256,512]{1,0:T(8,128)(2,1)S(1)} %bitcast.538), channel_id=1, source_target_pairs={{0,2},{2,0},{1,3},{3,1},{4,6},{6,4},{5,7},{7,5},{8,10},{10,8},{9,1... | collective-permute-start | bytes 786440 | tf_op jit(solution)/shard_map/ppermute | solution.py:267
  41.9 22.5 %collective-permute-start.2 = (bf16[256,1024]{1,0:T(8,128)(2,1)S(1)}, bf16[256,1024]{1,0:T(8,128)(2,1)S(1)}, u32[]{:S(2)}, u32[]{:S(2)}) collective-permute-start(bf16[256,1024]{1,0:T(8,128)(2,1)S(1)} %collective-permute-done), channel_id=1, source_target_pairs={{0,16},{16,0},{1,17},{17,1},{2,18},{18,2},{3,19},{19,3},{4,20},{20... | collective-permute-start | bytes 1572872 | tf_op jit(solution)/shard_map/ppermute | solution.py:267
  51.7 12.7 %collective-permute-start.3 = (bf16[256,1024]{1,0:T(8,128)(2,1)S(1)}, bf16[256,1024]{1,0:T(8,128)(2,1)S(1)}, u32[]{:S(2)}, u32[]{:S(2)}) collective-permute-start(bf16[256,1024]{1,0:T(8,128)(2,1)S(1)} %collective-permute-done.1), channel_id=1, source_target_pairs={{0,16},{16,0},{1,17},{17,1},{2,18},{18,2},{3,19},{19,3},{4,20},{20... | collective-permute-start | bytes 1572872 | tf_op jit(solution)/shard_map/ppermute | solution.py:267
  82.4 19.3 %collective-permute-start.19 = (bf16[256,512]{1,0:T(8,128)(2,1)S(1)}, bf16[256,512]{1,0:T(8,128)(2,1)S(1)}, u32[]{:S(2)}, u32[]{:S(2)}) collective-permute-start(bf16[256,512]{1,0:T(8,128)(2,1)S(1)} %get-tuple-element.196), channel_id=1, source_target_pairs={{0,8},{4,12},{8,0},{12,4},{1,9},{5,13},{9,1},{13,5},{2,10},{6,14},... | collective-permute-start | bytes 786440 | tf_op jit(solution)/shard_map/ppermute | solution.py:272
  85.7 32.7 %collective-permute-start.18 = (bf16[256,512]{1,0:T(8,128)(2,1)S(1)}, bf16[256,512]{1,0:T(8,128)(2,1)S(1)}, u32[]{:S(2)}, u32[]{:S(2)}) collective-permute-start(bf16[256,512]{1,0:T(8,128)(2,1)S(1)} %get-tuple-element.196), channel_id=1, source_target_pairs={{0,4},{4,8},{8,12},{12,0},{1,5},{5,9},{9,13},{13,1},{2,6},{6,10},{... | collective-permute-start | bytes 786440 | tf_op jit(solution)/shard_map/ppermute | solution.py:272
  85.7 39.2 %collective-permute-start.24 = (bf16[256,512]{1,0:T(8,128)(2,1)S(1)}, bf16[256,512]{1,0:T(8,128)(2,1)S(1)}, u32[]{:S(2)}, u32[]{:S(2)}) collective-permute-start(bf16[256,512]{1,0:T(8,128)(2,1)S(1)} %get-tuple-element.195), channel_id=1, source_target_pairs={{0,12},{4,0},{8,4},{12,8},{1,13},{5,1},{9,5},{13,9},{2,14},{6,2},{... | collective-permute-start | bytes 786440 | tf_op jit(solution)/shard_map/ppermute | solution.py:272
  91.2 36.5 %collective-permute-start.23 = (bf16[256,512]{1,0:T(8,128)(2,1)S(1)}, bf16[256,512]{1,0:T(8,128)(2,1)S(1)}, u32[]{:S(2)}, u32[]{:S(2)}) collective-permute-start(bf16[256,512]{1,0:T(8,128)(2,1)S(1)} %get-tuple-element.195), channel_id=1, source_target_pairs={{0,8},{4,12},{8,0},{12,4},{1,9},{5,13},{9,1},{13,5},{2,10},{6,14},... | collective-permute-start | bytes 786440 | tf_op jit(solution)/shard_map/ppermute | solution.py:272
  92.8 36.9 %collective-permute-start.22 = (bf16[256,512]{1,0:T(8,128)(2,1)S(1)}, bf16[256,512]{1,0:T(8,128)(2,1)S(1)}, u32[]{:S(2)}, u32[]{:S(2)}) collective-permute-start(bf16[256,512]{1,0:T(8,128)(2,1)S(1)} %get-tuple-element.195), channel_id=1, source_target_pairs={{0,4},{4,8},{8,12},{12,0},{1,5},{5,9},{9,13},{13,1},{2,6},{6,10},{... | collective-permute-start | bytes 786440 | tf_op jit(solution)/shard_map/ppermute | solution.py:272
  101.7 29.4 %collective-permute-start.13 = (bf16[256,1024]{0,1:T(8,128)(2,1)S(1)}, bf16[256,1024]{0,1:T(8,128)(2,1)S(1)}, u32[]{:S(2)}, u32[]{:S(2)}) collective-permute-start(bf16[256,1024]{0,1:T(8,128)(2,1)S(1)} %slice.1176), channel_id=1, source_target_pairs={{0,16},{16,0},{1,17},{17,1},{2,18},{18,2},{3,19},{19,3},{4,20},{20... | collective-permute-start | bytes 1572872 | tf_op jit(solution)/shard_map/ppermute | solution.py:267
  118.4 13.0 %collective-permute-start.15 = (bf16[256,1024]{0,1:T(8,128)(2,1)S(1)}, bf16[256,1024]{0,1:T(8,128)(2,1)S(1)}, u32[]{:S(2)}, u32[]{:S(2)}) collective-permute-start(bf16[256,1024]{0,1:T(8,128)(2,1)S(1)} %fusion.50), channel_id=1, source_target_pairs={{0,1},{1,0},{2,3},{3,2},{4,5},{5,4},{6,7},{7,6},{8,9},{9,8},{10,11... | collective-permute-start | bytes 1572872 | tf_op jit(solution)/shard_map/ppermute | solution.py:267
  124.9 16.1 %collective-permute-start.34 = (bf16[256,1024]{1,0:T(8,128)(2,1)S(1)}, bf16[256,1024]{1,0:T(8,128)(2,1)S(1)}, u32[]{:S(2)}, u32[]{:S(2)}) collective-permute-start(bf16[256,1024]{1,0:T(8,128)(2,1)S(1)} %copy-done.46), channel_id=1, source_target_pairs={{0,0},{2,16},{16,2},{18,18},{1,1},{3,17},{17,3},{19,19},{4,4},{6,2... | collective-permute-start | bytes 1572872 | tf_op jit(solution)/shard_map/ppermute | solution.py:528
  127.7 32.1 %collective-permute-start.21 = (bf16[1024,512]{1,0:T(8,128)(2,1)S(1)}, bf16[1024,512]{1,0:T(8,128)(2,1)S(1)}, u32[]{:S(2)}, u32[]{:S(2)}) collective-permute-start(bf16[1024,512]{1,0:T(8,128)(2,1)S(1)} %bitcast.526), channel_id=1, source_target_pairs={{0,2},{2,0},{1,3},{3,1},{4,6},{6,4},{5,7},{7,5},{8,10},{10,8},{9,1... | collective-permute-start | bytes 3145736 | tf_op jit(solution)/shard_map/ppermute | solution.py:267
  129.8 48.8 %collective-permute-start.25 = (bf16[1024,512]{1,0:T(8,128)(2,1)S(1)}, bf16[1024,512]{1,0:T(8,128)(2,1)S(1)}, u32[]{:S(2)}, u32[]{:S(2)}) collective-permute-start(bf16[1024,512]{1,0:T(8,128)(2,1)S(1)} %bitcast.527), channel_id=1, source_target_pairs={{0,2},{2,0},{1,3},{3,1},{4,6},{6,4},{5,7},{7,5},{8,10},{10,8},{9,1... | collective-permute-start | bytes 3145736 | tf_op jit(solution)/shard_map/ppermute | solution.py:267
  141.1 46.2 %collective-permute-start.35 = (bf16[2,256,256]{2,1,0:T(8,128)(2,1)S(1)}, bf16[2,256,256]{2,1,0:T(8,128)(2,1)S(1)}, u32[]{:S(2)}, u32[]{:S(2)}) collective-permute-start(bf16[2,256,256]{2,1,0:T(8,128)(2,1)S(1)} %pad_maximum_fusion.23), channel_id=1, source_target_pairs={{0,1},{1,0},{2,3},{3,2},{4,5},{5,4},{6,7},{7,6},{8,9},{9,8},{10,11... | collective-permute-start | bytes 786440 | tf_op jit(solution)/shard_map/ppermute | solution.py:267
  144.3 34.6 %collective-permute-start.28 = (bf16[256,1024]{0,1:T(8,128)(2,1)S(1)}, bf16[256,1024]{0,1:T(8,128)(2,1)S(1)}, u32[]{:S(2)}, u32[]{:S(2)}) collective-permute-start(bf16[256,1024]{0,1:T(8,128)(2,1)S(1)} %collective-permute-done.27), channel_id=1, source_target_pairs={{0,16},{16,0},{1,17},{17,1},{2,18},{18,2},{3,19},{19,3},{4,20},{20... | collective-permute-start | bytes 1572872 | tf_op jit(solution)/shard_map/ppermute | solution.py:267
  160.0 20.2 %collective-permute-start.16 = (bf16[256,1024]{0,1:T(8,128)(2,1)S(1)}, bf16[256,1024]{0,1:T(8,128)(2,1)S(1)}, u32[]{:S(2)}, u32[]{:S(2)}) collective-permute-start(bf16[256,1024]{0,1:T(8,128)(2,1)S(1)} %fusion.71), channel_id=1, source_target_pairs={{0,16},{16,0},{1,17},{17,1},{2,18},{18,2},{3,19},{19,3},{4,20},{20... | collective-permute-start | bytes 1572872 | tf_op jit(solution)/shard_map/ppermute | solution.py:267
  189.0 13.1 %collective-permute-start.30 = (bf16[256,1024]{0,1:T(8,128)(2,1)S(1)}, bf16[256,1024]{0,1:T(8,128)(2,1)S(1)}, u32[]{:S(2)}, u32[]{:S(2)}) collective-permute-start(bf16[256,1024]{0,1:T(8,128)(2,1)S(1)} %fusion.46), channel_id=1, source_target_pairs={{0,1},{1,0},{2,3},{3,2},{4,5},{5,4},{6,7},{7,6},{8,9},{9,8},{10,11... | collective-permute-start | bytes 1572872 | tf_op jit(solution)/shard_map/ppermute | solution.py:267
  204.8 21.5 %collective-permute-start.39 = (bf16[256,1024]{0,1:T(8,128)(2,1)}, bf16[256,1024]{0,1:T(8,128)(2,1)}, u32[]{:S(2)}, u32[]{:S(2)}) collective-permute-start(bf16[256,1024]{0,1:T(8,128)(2,1)} %get-tuple-element.147), channel_id=1, source_target_pairs={{0,1},{1,0},{2,3},{3,2},{4,5},{5,4},{6,7},{7,6},{8,9},{9,8},{10,11... | collective-permute-start | bytes 1572872 | tf_op jit(solution)/shard_map/ppermute | solution.py:267
  205.1 21.3 %collective-permute-start.37 = (bf16[256,1024]{0,1:T(8,128)(2,1)}, bf16[256,1024]{0,1:T(8,128)(2,1)}, u32[]{:S(2)}, u32[]{:S(2)}) collective-permute-start(bf16[256,1024]{0,1:T(8,128)(2,1)} %get-tuple-element.147), channel_id=1, source_target_pairs={{0,16},{16,0},{1,17},{17,1},{2,18},{18,2},{3,19},{19,3},{4,20},{20... | collective-permute-start | bytes 1572872 | tf_op jit(solution)/shard_map/ppermute | solution.py:267
  208.5 14.3 %collective-permute-start.31 = (bf16[2,256,256]{2,1,0:T(8,128)(2,1)}, bf16[2,256,256]{2,1,0:T(8,128)(2,1)}, u32[]{:S(2)}, u32[]{:S(2)}) collective-permute-start(bf16[2,256,256]{2,1,0:T(8,128)(2,1)} %get-tuple-element.193), channel_id=1, source_target_pairs={{0,1},{1,0},{2,3},{3,2},{4,5},{5,4},{6,7},{7,6},{8,9},{9,8},{10,11... | collective-permute-start | bytes 786440 | tf_op jit(solution)/shard_map/ppermute | solution.py:267
  234.8 29.5 %collective-permute-start.38 = (bf16[256,1024]{0,1:T(8,128)(2,1)}, bf16[256,1024]{0,1:T(8,128)(2,1)}, u32[]{:S(2)}, u32[]{:S(2)}) collective-permute-start(bf16[256,1024]{0,1:T(8,128)(2,1)} %slice.1172), channel_id=1, source_target_pairs={{0,16},{16,0},{1,17},{17,1},{2,18},{18,2},{3,19},{19,3},{4,20},{20... | collective-permute-start | bytes 1572872 | tf_op jit(solution)/shard_map/ppermute | solution.py:267
  236.2 118.4 %collective-permute-start.33 = (bf16[256,1024]{1,0:T(8,128)(2,1)}, bf16[256,1024]{1,0:T(8,128)(2,1)}, u32[]{:S(2)}, u32[]{:S(2)}) collective-permute-start(bf16[256,1024]{1,0:T(8,128)(2,1)} %pad_maximum_fusion.15), channel_id=1, source_target_pairs={{0,0},{2,16},{16,2},{18,18},{1,1},{3,17},{17,3},{19,19},{4,4},{6,2... | collective-permute-start | bytes 1572872 | tf_op jit(solution)/shard_map/ppermute | solution.py:621
  256.8 49.4 %collective-permute-start.64 = (bf16[4,264,512]{2,1,0:T(8,128)(2,1)S(1)}, bf16[4,264,512]{2,1,0:T(8,128)(2,1)S(1)}, u32[]{:S(2)}, u32[]{:S(2)}) collective-permute-start(bf16[4,264,512]{2,1,0:T(8,128)(2,1)S(1)} %dynamic-slice_convert_fusion), channel_id=1, source_target_pairs={{0,2},{2,0},{1,3},{3,1},{4,6},{6,4},{5,7},{7,5},{8,10},{10,8},{9,1... | collective-permute-start | bytes 3244040 | tf_op jit(solution)/shard_map/ppermute | solution.py:267
  259.5 13.6 %collective-permute-start.42 = (bf16[256,1024]{0,1:T(8,128)(2,1)S(1)}, bf16[256,1024]{0,1:T(8,128)(2,1)S(1)}, u32[]{:S(2)}, u32[]{:S(2)}) collective-permute-start(bf16[256,1024]{0,1:T(8,128)(2,1)S(1)} %fusion.43), channel_id=1, source_target_pairs={{0,1},{1,0},{2,3},{3,2},{4,5},{5,4},{6,7},{7,6},{8,9},{9,8},{10,11... | collective-permute-start | bytes 1572872 | tf_op jit(solution)/shard_map/ppermute | solution.py:267
  263.9 40.9 %collective-permute-start.60 = (bf16[4,256,512]{2,1,0:T(8,128)(2,1)S(1)}, bf16[4,256,512]{2,1,0:T(8,128)(2,1)S(1)}, u32[]{:S(2)}, u32[]{:S(2)}) collective-permute-start(bf16[4,256,512]{2,1,0:T(8,128)(2,1)S(1)} %dynamic-slice_convert_fusion.1), channel_id=1, source_target_pairs={{0,2},{2,0},{1,3},{3,1},{4,6},{6,4},{5,7},{7,5},{8,10},{10,8},{9,1... | collective-permute-start | bytes 3145736 | tf_op jit(solution)/shard_map/ppermute | solution.py:267
  276.3 70.9 %collective-permute-start.44 = (bf16[256,1024]{0,1:T(8,128)(2,1)}, bf16[256,1024]{0,1:T(8,128)(2,1)}, u32[]{:S(2)}, u32[]{:S(2)}) collective-permute-start(bf16[256,1024]{0,1:T(8,128)(2,1)} %get-tuple-element.130), channel_id=1, source_target_pairs={{0,1},{1,0},{2,3},{3,2},{4,5},{5,4},{6,7},{7,6},{8,9},{9,8},{10,11... | collective-permute-start | bytes 1572872 | tf_op jit(solution)/shard_map/ppermute | solution.py:267
  305.5 22.0 %collective-permute-start.62 = (bf16[256,512]{1,0:T(8,128)(2,1)S(1)}, bf16[256,512]{1,0:T(8,128)(2,1)S(1)}, u32[]{:S(2)}, u32[]{:S(2)}) collective-permute-start(bf16[256,512]{1,0:T(8,128)(2,1)S(1)} %get-tuple-element.166), channel_id=1, source_target_pairs={{0,8},{4,12},{8,0},{12,4},{1,9},{5,13},{9,1},{13,5},{2,10},{6,14},... | collective-permute-start | bytes 786440 | tf_op jit(solution)/shard_map/ppermute | solution.py:272
  306.3 35.2 %collective-permute-start.61 = (bf16[256,512]{1,0:T(8,128)(2,1)S(1)}, bf16[256,512]{1,0:T(8,128)(2,1)S(1)}, u32[]{:S(2)}, u32[]{:S(2)}) collective-permute-start(bf16[256,512]{1,0:T(8,128)(2,1)S(1)} %get-tuple-element.164), channel_id=1, source_target_pairs={{0,12},{4,0},{8,4},{12,8},{1,13},{5,1},{9,5},{13,9},{2,14},{6,2},{... | collective-permute-start | bytes 786440 | tf_op jit(solution)/shard_map/ppermute | solution.py:272
  312.5 32.4 %collective-permute-start.67 = (bf16[264,512]{1,0:T(8,128)(2,1)S(1)}, bf16[264,512]{1,0:T(8,128)(2,1)S(1)}, u32[]{:S(2)}, u32[]{:S(2)}) collective-permute-start(bf16[264,512]{1,0:T(8,128)(2,1)S(1)} %get-tuple-element.149), channel_id=1, source_target_pairs={{0,4},{4,8},{8,12},{12,0},{1,5},{5,9},{9,13},{13,1},{2,6},{6,10},{... | collective-permute-start | bytes 811016 | tf_op jit(solution)/shard_map/ppermute | solution.py:272
  327.5 23.2 %collective-permute-start.66 = (bf16[264,512]{1,0:T(8,128)(2,1)S(1)}, bf16[264,512]{1,0:T(8,128)(2,1)S(1)}, u32[]{:S(2)}, u32[]{:S(2)}) collective-permute-start(bf16[264,512]{1,0:T(8,128)(2,1)S(1)} %get-tuple-element.150), channel_id=1, source_target_pairs={{0,8},{4,12},{8,0},{12,4},{1,9},{5,13},{9,1},{13,5},{2,10},{6,14},... | collective-permute-start | bytes 811016 | tf_op jit(solution)/shard_map/ppermute | solution.py:272
  344.9 21.9 %collective-permute-start.43 = (bf16[256,1024]{0,1:T(8,128)(2,1)}, bf16[256,1024]{0,1:T(8,128)(2,1)}, u32[]{:S(2)}, u32[]{:S(2)}) collective-permute-start(bf16[256,1024]{0,1:T(8,128)(2,1)} %get-tuple-element.130), channel_id=1, source_target_pairs={{0,16},{16,0},{1,17},{17,1},{2,18},{18,2},{3,19},{19,3},{4,20},{20... | collective-permute-start | bytes 1572872 | tf_op jit(solution)/shard_map/ppermute | solution.py:267
  347.2 19.5 %collective-permute-start.45 = (bf16[256,1024]{0,1:T(8,128)(2,1)}, bf16[256,1024]{0,1:T(8,128)(2,1)}, u32[]{:S(2)}, u32[]{:S(2)}) collective-permute-start(bf16[256,1024]{0,1:T(8,128)(2,1)} %collective-permute-done.44), channel_id=1, source_target_pairs={{0,16},{16,0},{1,17},{17,1},{2,18},{18,2},{3,19},{19,3},{4,20},{20... | collective-permute-start | bytes 1572872 | tf_op jit(solution)/shard_map/ppermute | solution.py:267
  363.6 33.7 %collective-permute-start.69 = (bf16[2,520,256]{2,1,0:T(8,128)(2,1)}, bf16[2,520,256]{2,1,0:T(8,128)(2,1)}, u32[]{:S(2)}, u32[]{:S(2)}) collective-permute-start(bf16[2,520,256]{2,1,0:T(8,128)(2,1)} %pad_maximum_fusion.13), channel_id=1, source_target_pairs={{0,16},{16,0},{1,17},{17,1},{2,18},{18,2},{3,19},{19,3},{4,20},{20... | collective-permute-start | bytes 1597448 | tf_op jit(solution)/shard_map/ppermute | solution.py:267
  388.9 42.1 %collective-permute-start.47 = (bf16[256,1024]{1,0:T(8,128)(2,1)}, bf16[256,1024]{1,0:T(8,128)(2,1)}, u32[]{:S(2)}, u32[]{:S(2)}) collective-permute-start(bf16[256,1024]{1,0:T(8,128)(2,1)} %convolution_convert_fusion.1), channel_id=1, source_target_pairs={{0,16},{16,0},{1,17},{17,1},{2,18},{18,2},{3,19},{19,3},{4,20},{20... | collective-permute-start | bytes 1572872 | tf_op jit(solution)/shard_map/ppermute | solution.py:267
  394.3 34.2 %collective-permute-start.54 = (bf16[4,200,512]{2,1,0:T(8,128)(2,1)S(1)}, bf16[4,200,512]{2,1,0:T(8,128)(2,1)S(1)}, u32[]{:S(2)}, u32[]{:S(2)}) collective-permute-start(bf16[4,200,512]{2,1,0:T(8,128)(2,1)S(1)} %dynamic-slice_convert_fusion.2), channel_id=1, source_target_pairs={{0,2},{2,0},{1,3},{3,1},{4,6},{6,4},{5,7},{7,5},{8,10},{10,8},{9,1... | collective-permute-start | bytes 2457608 | tf_op jit(solution)/shard_map/ppermute | solution.py:267
  395.0 24.3 %collective-permute-start.50 = (bf16[4,64,512]{2,1,0:T(8,128)(2,1)S(1)}, bf16[4,64,512]{2,1,0:T(8,128)(2,1)S(1)}, u32[]{:S(2)}, u32[]{:S(2)}) collective-permute-start(bf16[4,64,512]{2,1,0:T(8,128)(2,1)S(1)} %dynamic-slice_convert_fusion.3), channel_id=1, source_target_pairs={{0,2},{2,0},{1,3},{3,1},{4,6},{6,4},{5,7},{7,5},{8,10},{10,8},{9,1... | collective-permute-start | bytes 786440 | tf_op jit(solution)/shard_map/ppermute | solution.py:267
  424.0 32.1 %collective-permute-start.46 = (bf16[256,1024]{1,0:T(8,128)(2,1)}, bf16[256,1024]{1,0:T(8,128)(2,1)}, u32[]{:S(2)}, u32[]{:S(2)}) collective-permute-start(bf16[256,1024]{1,0:T(8,128)(2,1)} %convolution_convert_fusion.2), channel_id=1, source_target_pairs={{0,16},{16,0},{1,17},{17,1},{2,18},{18,2},{3,19},{19,3},{4,20},{20... | collective-permute-start | bytes 1572872 | tf_op jit(solution)/shard_map/ppermute | solution.py:267
  429.0 16.9 %collective-permute-start.56 = (bf16[200,512]{1,0:T(8,128)(2,1)S(1)}, bf16[200,512]{1,0:T(8,128)(2,1)S(1)}, u32[]{:S(2)}, u32[]{:S(2)}) collective-permute-start(bf16[200,512]{1,0:T(8,128)(2,1)S(1)} %get-tuple-element.173), channel_id=1, source_target_pairs={{0,8},{4,12},{8,0},{12,4},{1,9},{5,13},{9,1},{13,5},{2,10},{6,14},... | collective-permute-start | bytes 614408 | tf_op jit(solution)/shard_map/ppermute | solution.py:272
  431.0 18.7 %collective-permute-start.55 = (bf16[200,512]{1,0:T(8,128)(2,1)S(1)}, bf16[200,512]{1,0:T(8,128)(2,1)S(1)}, u32[]{:S(2)}, u32[]{:S(2)}) collective-permute-start(bf16[200,512]{1,0:T(8,128)(2,1)S(1)} %get-tuple-element.171), channel_id=1, source_target_pairs={{0,12},{4,0},{8,4},{12,8},{1,13},{5,1},{9,5},{13,9},{2,14},{6,2},{... | collective-permute-start | bytes 614408 | tf_op jit(solution)/shard_map/ppermute | solution.py:272
  433.5 22.6 %collective-permute-start.48 = (bf16[256,1024]{1,0:T(8,128)(2,1)}, bf16[256,1024]{1,0:T(8,128)(2,1)S(1)}, u32[]{:S(2)}, u32[]{:S(2)}) collective-permute-start(bf16[256,1024]{1,0:T(8,128)(2,1)} %add_convert_fusion.1), channel_id=1, source_target_pairs={{0,1},{1,0},{2,3},{3,2},{4,5},{5,4},{6,7},{7,6},{8,9},{9,8},{10,11... | collective-permute-start | bytes 1572872 | tf_op jit(solution)/shard_map/ppermute | solution.py:267
  (84 other events, 836.9 us)

commit v2 on v0

--- a/solution.py
+++ b/solution.py
@@ -1,6 +1,9 @@
 import jax
 import jax.numpy as jnp
 from jax import lax
+from jax.experimental import pallas as pl
+from jax.experimental.pallas import tpu as pltpu
+from jax.sharding import Mesh
 from jax.sharding import PartitionSpec as P
 
 D = 1024
@@ -254,42 +257,862 @@
     )
 
 
+BF = jnp.bfloat16
+F32 = jnp.float32
+PAIR = ((0, 1), (1, 0))
+MEBIBYTE = 1024 * 1024
+BLOCK = 256
+
+
+def flip(values, axis_name):
+    return lax.ppermute(values, axis_name, PAIR)
+
+
+def shift(values, axis_name, step):
+    size = lax.axis_size(axis_name)
+    return lax.ppermute(values, axis_name, [(i, (i + step) % size) for i in range(size)])
+
+
+def in_order(index, mine, other, axis):
+    first = jnp.where(index == 0, mine, other)
+    second = jnp.where(index == 0, other, mine)
+    return jnp.concatenate([first, second], axis)
+
+
+def four_in_order(low_bit, high_bit, parts, axis):
+    low = [jnp.where(low_bit == 0, parts[i], parts[i ^ 1]) for i in range(4)]
+    full = [jnp.where(high_bit == 0, low[i], low[i ^ 2]) for i in range(4)]
+    return jnp.concatenate(full, axis)
+
+
+def cut(values, index, size, axis):
+    return lax.dynamic_slice_in_dim(values, index * size, size, axis)
+
+
+def after(values, *earlier):
+    return lax.optimization_barrier((values, earlier))[0]
+
+
+def part(index, size):
+    return pl.ds(pl.multiple_of(index * size, size), size)
+
+
+def kernel_call(kernel, name, outs, places, *inputs, grid=1, specs=None, out_specs=None, scratch=(), vmem=16):
+    return pl.pallas_call(
+        kernel,
+        grid_spec=pltpu.PrefetchScalarGridSpec(
+            num_scalar_prefetch=1,
+            grid=(grid,),
+            in_specs=[fixed(x.shape) for x in inputs] if specs is None else specs,
+            out_specs=[fixed(shape) for shape, _ in outs] if out_specs is None else out_specs,
+            scratch_shapes=list(scratch),
+        ),
+        out_shape=[jax.ShapeDtypeStruct(shape, dtype) for shape, dtype in outs],
+        compiler_params=pltpu.CompilerParams(vmem_limit_bytes=vmem * MEBIBYTE),
+        cost_estimate=pl.CostEstimate(flops=1, bytes_accessed=1, transcendentals=0),
+        name=name,
+    )(places, *inputs)
+
+
+def fixed(shape):
+    return pl.BlockSpec(shape, lambda step, places: (0,) * len(shape))
+
+
+def stepped(shape, axis):
+    return pl.BlockSpec(
+        shape, lambda step, places: tuple(step if i == axis else 0 for i in range(len(shape)))
+    )
+
+
+def prepare_attn_kernel(places, w_qkv, b_qv, w_out, *refs):
+    vectors, (keep, send, turned) = refs[:-3], refs[-3:]
+    head = turned.shape[1] // 4
+    for piece in range(3):
+        turned[piece] = w_qkv[piece].T
+    for ref, quarter in ((keep, places[0]), (send, places[1])):
+        for piece in range(3):
+            ref[piece * head : (piece + 1) * head] = turned[piece, part(quarter, head), :]
+        bias = b_qv[...].astype(F32)
+        own = sum(
+            jnp.where(quarter == q, bias[:, q * head : (q + 1) * head], 0.0) for q in range(4)
+        )
+        line = jnp.concatenate([own[0:1], own[1:2]], 1)
+        line = jnp.concatenate([line, jnp.zeros((1, keep.shape[1] - 2 * head), F32)], 1)
+        rows = [jnp.broadcast_to(line, (8, keep.shape[1]))]
+        rows += [vector[...].astype(F32).reshape(1, -1) for vector in vectors]
+        rows += [jnp.zeros((2, keep.shape[1]), F32)]
+        ref[3 * head : 3 * head + 16] = jnp.concatenate(rows, 0).astype(BF)
+        ref[3 * head + 16 :] = w_out[part(quarter, head), :]
+
+
+def prepare_ff_kernel(places, w_up, w_down, keep, send):
+    for ref, quarter in ((keep, places[0]), (send, places[1])):
+        ref[:BLOCK] = w_up[:, part(quarter, BLOCK)].T
+        ref[BLOCK:] = w_down[part(quarter, BLOCK), :]
+
+
+def attend_kernel(places, x00, x01, x10, x11, own, far, qkv_ref, out_ref, norm_ref, *weight_refs):
+    head_rows = qkv_ref.shape[2]
+    total = None
+    for side, pair in ((0, (x00, x01)), (1, (x10, x11))):
+        mine = (places[3] ^ side) == places[2]
+        for end, x in enumerate(pair):
+            weight = jnp.where(mine, own[0, end, : 3 * head_rows], far[0, end, : 3 * head_rows])
+            weight_refs[2 * side + end][0] = weight
+            piece = matmul(weight, x[...])
+            total = piece if total is None else total + piece
+    bias = own[0, 0, 3 * head_rows : 3 * head_rows + 8].astype(F32)[0:1, : 2 * head_rows]
+    bias = jnp.broadcast_to(bias, (2 * head_rows, 2 * head_rows)).T
+    query = (total[:head_rows] + bias[:head_rows, 0:1]) * HEAD_DIM**-0.5
+    qkv_ref[0, 0] = query.astype(BF)
+    key = total[head_rows : 2 * head_rows].astype(BF)
+    qkv_ref[0, 1] = key
+    value = (total[2 * head_rows :] + bias[head_rows:, 0:1]).astype(BF)
+    qkv_ref[0, 2] = value
+    key_t = key.T
+    for start in range(0, SEQ, BLOCK):
+        here = slice(start, start + BLOCK)
+        scores = matmul(key_t, qkv_ref[0, 0, :, here])
+        top = jnp.max(scores, axis=0, keepdims=True)
+        weights = jnp.exp(scores - top)
+        denom = jnp.sum(weights, axis=0, keepdims=True)
+        out_ref[0, :, here] = matmul(value, weights.astype(BF)) * (1.0 / denom)
+        norm_ref[0, :, here] = top + jnp.log(denom)
+
+
+def turn_kernel(places, *refs):
+    for ref, out_ref in zip(refs[:4], refs[4:]):
+        out_ref[...] = ref[...].T
+
+
+def out_far_kernel(places, attended, mixed, other, own_ref, send_ref, full_ref, low_ref):
+    heads, head_rows, _ = attended.shape
+    half = other.shape[2]
+    low_ref[...] = attended[...].astype(BF)
+    for head in range(heads):
+        source = lax.rem(places[5] - head + heads, heads)
+        rows = slice(head * head_rows, (head + 1) * head_rows)
+        full_ref[rows, part(places[2], half)] = mixed[source, 8 : 8 + head_rows, :]
+        full_ref[rows, part(1 - places[2], half)] = other[source, 8:, :]
+    out_block(places, 3, low_ref, full_ref, send_ref)
+    out_block(places, 2, low_ref, full_ref, own_ref)
+
+
+def out_near_kernel(places, attended, full_ref, own_ref, send_ref):
+    out_block(places, 1, attended, full_ref, send_ref)
+    out_block(places, 0, attended, full_ref, own_ref)
+
+
+def out_block(places, step, attended, full_ref, out_ref):
+    rows = attended[:, :, part(places[0] ^ step, BLOCK)].reshape(-1, BLOCK)
+    out_ref[...] = inner_rows(rows, full_ref[...]).astype(out_ref.dtype)
+
+
+def norm1_kernel(places, near, core, got, x00, x01, x10, x11, vec, a_ref, low_ref, normed_ref, scale_ref):
+    for side, pair in ((0, (x00, x01)), (1, (x10, x11))):
+        for end, x in enumerate(pair):
+            block = 2 * (places[3] ^ side) + (places[4] ^ end)
+            a_ref[:, part(block, BLOCK)] = x[...].T.astype(F32)
+    residual = a_ref[...] + (near[...] + core[...].astype(F32) + got[...].astype(F32) + vec[0:1])
+    mean_rows = jnp.mean(residual, axis=1, keepdims=True)
+    spread = jnp.mean(residual * residual, axis=1, keepdims=True) - mean_rows * mean_rows
+    scale_rows = lax.rsqrt(spread + norm_eps)
+    normed = (residual - mean_rows) * scale_rows
+    values = normed * vec[1:2] + vec[2:3]
+    a_ref[...] = values
+    low_ref[...] = values.astype(BF)
+    normed_ref[...] = normed
+    scale_ref[...] = scale_rows
+
+
+def back_of_norm(grad_in, normed, scale_rows, gain_vec):
+    scaled = grad_in * gain_vec
+    first = jnp.mean(scaled, axis=1, keepdims=True)
+    second = jnp.mean(scaled * normed, axis=1, keepdims=True)
+    return scale_rows * (scaled - first - normed * second)
+
+
+def add_sums(sums_ref, *arrays):
+    @pl.when(pl.program_id(0) == 0)
+    def _():
+        sums_ref[...] = jnp.zeros_like(sums_ref)
+
+    for index, values in enumerate(arrays):
+        sums_ref[index : index + 1] += jnp.sum(values, axis=0, keepdims=True)
+
+
+def norm2_kernel(places, near, core, got, a_ref, c0, c1, c2, c3, vec, here_ref, send_ref, grad_ref, low_ref, sums_ref):
+    for index, piece in enumerate((c0, c1, c2, c3)):
+        block = 2 * (places[3] ^ (index >> 1)) + (places[4] ^ (index & 1))
+        grad_ref[:, part(block, BLOCK)] = piece[...].T.astype(F32)
+    branch = near[...] + core[...].astype(F32) + got[...].astype(F32) + vec[3:4]
+    residual = a_ref[...] + branch
+    mean_rows = jnp.mean(residual, axis=1, keepdims=True)
+    spread = jnp.mean(residual * residual, axis=1, keepdims=True) - mean_rows * mean_rows
+    scale_rows = lax.rsqrt(spread + norm_eps)
+    normed = (residual - mean_rows) * scale_rows
+    grad_out = grad_ref[...]
+    grad = back_of_norm(grad_out, normed, scale_rows, vec[4:5])
+    add_sums(sums_ref, grad, grad_out * normed, grad_out)
+    grad_ref[...] = normed * vec[4:5] + vec[5:6]
+    for side in range(2):
+        for end, ref in ((0, here_ref), (1, send_ref)):
+            block = 2 * (places[3] ^ side) + (places[4] ^ end)
+            ref[side] = grad_ref[:, part(block, BLOCK)].T.astype(BF)
+    grad_ref[...] = grad
+    low_ref[...] = grad.astype(BF)
+
+
+def norm1_back_kernel(places, near, core, got, grad2, normed_ref, scale_ref, vec, sums2, low_ref, sums_ref):
+    grad_in = grad2[...] + (near[...] + core[...].astype(F32) + got[...].astype(F32))
+    normed = normed_ref[...]
+    grad = back_of_norm(grad_in, normed, scale_ref[...], vec[1:2])
+    add_sums(sums_ref, grad, grad_in * normed, grad_in)
+    sums_ref[3:6] = sums2[0:3]
+    low_ref[...] = grad.astype(BF)
+
+
+def weight_grad_kernel(places, left_near, left_far, r0, r1, r2, r3, mine_ref, sent_ref, right):
+    half = mine_ref.shape[2]
+
+    @pl.when(pl.program_id(0) == 0)
+    def _():
+        for index, rows in enumerate((r0, r1, r2, r3)):
+            here = slice(index * BLOCK, (index + 1) * BLOCK)
+            right[0, here] = rows[:, part(places[2], half)]
+            right[1, here] = rows[:, part(1 - places[2], half)]
+
+    left = jnp.concatenate([left_near[...], left_far[...]], 0)
+    sent_ref[0, :BLOCK] = inner_rows(left, right[1]).astype(BF)
+    mine_ref[0, :BLOCK] = inner_rows(left, right[0]).astype(BF)
+    if mine_ref.shape[1] > BLOCK:
+        sums = jnp.sum(left.astype(F32), axis=0, keepdims=True)
+        sums = jnp.broadcast_to(jnp.concatenate([sums, sums], 1), (8, half)).astype(BF)
+        sent_ref[0, BLOCK:] = sums
+        mine_ref[0, BLOCK:] = sums
+
+
+def out_back_kernel(places, d0, d1, d2, d3, full_ref, attended, grad_ref, mine_ref, sent_ref):
+    heads, head_rows, _ = attended.shape
+    blocks = (d0, d1, d2, d3)
+    left = []
+    for step, rows in enumerate(blocks):
+        here = part(places[0] ^ step, BLOCK)
+        grad = against(full_ref[...], rows[...]).astype(BF)
+        grad_ref[:, :, here] = grad.reshape(heads, head_rows, BLOCK)
+        left.append(attended[:, :, here].reshape(-1, BLOCK))
+    width = mine_ref.shape[3]
+    for ref, side in ((sent_ref, 1 - places[2]), (mine_ref, places[2])):
+        for end in range(2):
+            columns = part(2 * side + (places[4] ^ end), width)
+            total = None
+            for piece, rows in zip(left, blocks):
+                product = matmul(piece, rows[:, columns])
+                total = product if total is None else total + product
+            ref[:, end] = total.astype(BF).reshape(heads, head_rows, width)
+
+
+def attend_back_kernel(
+    places, qkv_ref, grad_ref, norm_ref, attended, x00, x01, x10, x11, sums, out_ref, mine_ref, sent_ref, probs_low, scores_low
+):
+    head_rows = qkv_ref.shape[2]
+    key = qkv_ref[0, 1]
+    key_t = key.T
+    value_t = qkv_ref[0, 2].T
+    for start in range(0, SEQ, BLOCK):
+        here = slice(start, start + BLOCK)
+        grad = grad_ref[0, :, here]
+        probs = jnp.exp(matmul(key_t, qkv_ref[0, 0, :, here]) - norm_ref[0, :, here])
+        delta = jnp.sum(grad.astype(F32) * attended[0, :, here], axis=0, keepdims=True)
+        grad_scores = (probs * (matmul(value_t, grad) - delta)).astype(BF)
+        probs_low[:, here] = probs.astype(BF)
+        scores_low[:, here] = grad_scores
+        grad_query = matmul(key, grad_scores).astype(BF)
+        out_ref[0, :head_rows, here] = (grad_query.astype(F32) * HEAD_DIM**-0.5).astype(BF)
+    grad_key = matmul(scores_low[...], qkv_ref[0, 0].T)
+    out_ref[0, head_rows : 2 * head_rows] = grad_key.T.astype(BF)
+    grad_value = matmul(probs_low[...], grad_ref[0].T)
+    out_ref[0, 2 * head_rows :] = grad_value.T.astype(BF)
+    left = out_ref[0]
+    bias = jnp.sum(left.astype(F32), axis=1, keepdims=True)
+    bias = jnp.concatenate([bias[:head_rows], bias[2 * head_rows :]], 0)
+    bias = jnp.broadcast_to(bias, (2 * head_rows, 2 * head_rows)).T[:8]
+    bias = jnp.concatenate([bias, jnp.zeros((8, BLOCK - 2 * head_rows), F32)], 1)
+    rows = 3 * head_rows
+    for side, pair in ((0, (x00, x01)), (1, (x10, x11))):
+        mine = (places[3] ^ side) == places[2]
+        for end, x in enumerate(pair):
+            weight = matmul(left, x[...]).astype(BF)
+            block = sums[:, part(2 * (places[3] ^ side) + (places[4] ^ end), BLOCK)]
+            extra = jnp.concatenate([block, bias], 0).astype(BF)
+
+            @pl.when(mine)
+            def _():
+                mine_ref[0, end, :rows] = weight
+                mine_ref[0, end, rows:] = extra
+
+            @pl.when(jnp.logical_not(mine))
+            def _():
+                sent_ref[0, end, :rows] = weight
+                sent_ref[0, end, rows:] = extra
+
+
+def both_halves(mine, got, out_mine, out_got, head, place):
+    sums = mine[head].astype(F32) + got[head].astype(F32)
+    outs = out_mine[place].astype(F32) + out_got[place].astype(F32)
+    return jnp.concatenate([sums, outs], 1)
+
+
+def late_sum_kernel(places, mine, got, out_mine, out_got, *sums):
+    for head, ref in enumerate(sums):
+        place = head + out_mine.shape[0] - len(sums)
+        ref[...] = both_halves(mine, got, out_mine, out_got, head, place).astype(BF)
+
+
+def early_sum_kernel(places, mine, got, out_mine, out_got, own_ref, *sums):
+    own_ref[...] = both_halves(mine, got, out_mine, out_got, 0, 0)
+    for head, ref in enumerate(sums):
+        ref[...] = both_halves(mine, got, out_mine, out_got, head + 1, head + 1).astype(BF)
+
+
+def last_sum_kernel(places, own_ref, *refs):
+    total = own_ref[...]
+    for ref in refs[:-2]:
+        total = total + ref[...].astype(F32)
+    refs[-2][...] = total[0].astype(BF)
+    refs[-1][...] = total[1].astype(BF)
+
+
+def input_near_kernel(places, weight_own, weight_send, grads, d0, d1, d2, d3, own_ref, send_ref):
+    heads, rows, _ = grads.shape
+    right = grads[...].reshape(heads * rows, SEQ)
+    send_ref[...] = inner_rows(weight_send[...].reshape(heads * rows, -1), right).astype(BF)
+    own_ref[...] = inner_rows(weight_own[...].reshape(heads * rows, -1), right)
+    block = 2 * places[3] + places[4]
+    for step, d in enumerate((d0, d1, d2, d3)):
+        here = part(places[0] ^ step, BLOCK)
+        own_ref[:, here] += d[:, part(block, BLOCK)].T.astype(F32)
+
+
+def last_attn_kernel(places, p0, p1, p2, p3, qkv_out, qv_out, norm_out, out_out, turned):
+    parts = (p0, p1, p2, p3)
+    head = turned.shape[0] // 4
+    for piece in range(3):
+        for step, ref in enumerate(parts):
+            turned[part(places[0] ^ step, head), :] = ref[piece * head : (piece + 1) * head].astype(F32)
+        qkv_out[piece] = turned[...].T
+    extra = [ref[3 * head : 3 * head + 16].astype(F32) for ref in parts]
+    norm_out[...] = extra[0][:8] + extra[1][:8] + extra[2][:8] + extra[3][:8]
+    lines = [[], []]
+    for quarter in range(4):
+        line = sum(
+            jnp.where((places[0] ^ step) == quarter, extra[step][8:9], 0.0) for step in range(4)
+        )
+        lines[0].append(line[:, :head])
+        lines[1].append(line[:, head : 2 * head])
+    qv_out[...] = jnp.concatenate([jnp.concatenate(line, 1) for line in lines], 0)
+    for step, ref in enumerate(parts):
+        out_out[part(places[0] ^ step, head), :] = ref[3 * head + 16 :].astype(F32)
+
+
+def last_up_kernel(places, p0, p1, p2, p3, up_out, bias_out):
+    for step, ref in enumerate((p0, p1, p2, p3)):
+        quarter = places[0] ^ step
+        up_out[:, part(quarter, BLOCK)] = ref[:BLOCK].astype(F32).T
+        bias_out[:, part(quarter, BLOCK)] = ref[BLOCK:].astype(F32)[0:1]
+
+
+def last_down_kernel(places, p0, p1, p2, p3, down_out):
+    for step, ref in enumerate((p0, p1, p2, p3)):
+        down_out[part(places[0] ^ step, BLOCK), :] = ref[...].astype(F32)
+
+
+def to_far_chip(own, send):
+    return (own + flip(send, "dp").astype(F32)).astype(BF)
+
+
+def gather_rows(payload):
+    size = lax.axis_size("row")
+    return jnp.stack([payload] + [shift(payload, "row", step) for step in range(1, size)])
+
+
+def gather_blocks(payload):
+    return lax.all_gather(payload, "row", axis=0)
+
+
+def reduce_blocks(both):
+    return lax.psum_scatter(both.astype(BF), "row", scatter_dimension=0)
+
+
+def spread_weights(mine, other):
+    near = jnp.stack([mine, flip(other, "t")])
+    far = flip(near, "dp")
+    return near[0], far[0], near[1], far[1]
+
+
+def fast_shards(
+    tokens,
+    w_qkv,
+    b_qv,
+    w_out,
+    b_out,
+    norm1_gain,
+    norm1_shift,
+    w_up,
+    b_up,
+    w_down,
+    b_down,
+    norm2_gain,
+    norm2_shift,
+    cotangent,
+):
+    core, chip = lax.axis_index("dp"), lax.axis_index("t")
+    u_index, row = lax.axis_index("u"), lax.axis_index("row")
+    rows = lax.axis_size("row")
+    quarter = 2 * chip + core
+    other_quarter = 2 * (1 - chip) + core
+    places = jnp.stack([quarter, other_quarter, u_index, core, chip, row]).astype(jnp.int32)
+    feats = tokens.shape[0]
+    width = 4 * feats
+    half = 2 * feats
+    own_rows = SEQ // 4
+    swap_cores = [(2 * d + u, 2 * u + d) for d in range(2) for u in range(2)]
+    head_rows = w_out.shape[0] // 4
+    qkv_rows, out_rows, ff_rows = 3 * head_rows, head_rows, w_down.shape[0] // 4
+
+    x00 = lax.ppermute(tokens, ("dp", "u"), swap_cores)
+
+    attn_rows = qkv_rows + 16 + out_rows
+    attn_keep, attn_send = kernel_call(
+        prepare_attn_kernel,
+        "prepare_attn",
+        [((attn_rows, feats), BF)] * 2,
+        places,
+        w_qkv.transpose(1, 0, 2),
+        b_qv,
+        w_out,
+        b_out,
+        norm1_gain,
+        norm1_shift,
+        b_down,
+        norm2_gain,
+        norm2_shift,
+        scratch=[pltpu.VMEM((3, 4 * head_rows, feats), BF)],
+        vmem=60,
+    )
+    attn_got = flip(attn_send, "t")
+    ff_keep, ff_send = kernel_call(
+        prepare_ff_kernel, "prepare_ff", [((2 * ff_rows, feats), BF)] * 2, places, after(w_up, attn_send), w_down, vmem=60
+    )
+    ff_got = flip(ff_send, "t")
+    attn_got = after(attn_got, x00)
+    cot = lax.ppermute(after(cotangent, x00), ("dp", "u"), swap_cores)
+    x01 = flip(x00, "t")
+    x10, x11 = flip(x00, "dp"), flip(x01, "dp")
+    cot = after(cot, x01)
+    cot_parts = [cut(cot, quarter ^ j, own_rows, 1) for j in range(4)]
+    cot_far = flip(jnp.stack([cot_parts[2], cot_parts[3]]), "t")
+    cot_near = flip(jnp.stack([cot_parts[1], cot_far[1]]), "dp")
+
+    qkv_part = jnp.stack([attn_keep[: qkv_rows + 8], attn_got[: qkv_rows + 8]])
+    qkv_part, ff_got = lax.optimization_barrier((qkv_part, ff_got))
+    qkv_own = gather_rows(qkv_part)
+    attn_both = in_order(chip, attn_keep[qkv_rows + 8 :], attn_got[qkv_rows + 8 :], 1)
+    ff_both = in_order(chip, ff_keep, ff_got, 1)
+    up_bias = lax.dynamic_index_in_dim(b_up.reshape(4, -1), quarter, 0, True)
+    up_bias = jnp.pad(up_bias, ((0, 7), (0, half - ff_rows)))
+    down_both = in_order(u_index, ff_both[ff_rows:], flip(ff_both[ff_rows:], "u"), 1)
+    mixed = gather_blocks(jnp.concatenate([attn_both, ff_both[:ff_rows], up_bias]))
+    down_full = gather_blocks(down_both).reshape(rows * ff_rows, width)
+    qkv_far = flip(after(qkv_own, x01, down_both), "u")
+
+    x_blocks = (x00, x01, x10, x11)
+    qkv, attended, log_norm, *weight = kernel_call(
+        attend_kernel,
+        "attend",
+        [
+            ((rows, 3, head_rows, SEQ), BF),
+            ((rows, head_rows, SEQ), F32),
+            ((rows, 1, SEQ), F32),
+        ]
+        + [((rows, qkv_rows, feats), BF)] * 4,
+        places,
+        *x_blocks,
+        qkv_own,
+        qkv_far,
+        grid=rows,
+        specs=[fixed((feats, SEQ))] * 4 + [stepped((1, 2, qkv_rows + 8, feats), 0)] * 2,
+        out_specs=[
+            stepped((1, 3, head_rows, SEQ), 0),
+            stepped((1, head_rows, SEQ), 0),
+            stepped((1, 1, SEQ), 0),
+        ]
+        + [stepped((1, qkv_rows, feats), 0)] * 4,
+        vmem=28,
+    )
+    mixed = after(mixed, qkv_far, cot_near)
+    vec_rows = 8 + out_rows
+    out_other = flip(mixed[:, :vec_rows], "u")
+    up_own = mixed[:, vec_rows : vec_rows + ff_rows]
+    up_far = flip(after(up_own, out_other), "u")
+    bias_up = mixed[:, vec_rows + ff_rows, :ff_rows].reshape(1, -1).astype(F32)
+    vec = in_order(u_index, mixed[0, :8], out_other[0, :8], 1).astype(F32)
+    up_full = in_order(
+        u_index, up_own.reshape(rows * ff_rows, half), up_far.reshape(rows * ff_rows, half), 1
+    )
+
+    row_block = (own_rows, width)
+    pair_outs = [(row_block, F32), (row_block, BF)]
+    far_own, far_send, out_full, low_attended = kernel_call(
+        out_far_kernel,
+        "out_far",
+        pair_outs + [((rows * head_rows, width), BF), (attended.shape, BF)],
+        places,
+        attended,
+        mixed,
+        out_other,
+        specs=[fixed(attended.shape), fixed((rows, vec_rows, half)), fixed(out_other.shape)],
+    )
+    sent = to_far_chip(far_own, far_send)
+    near_attended = after(low_attended, sent)
+    got = flip(sent, "t")
+    near_own, near_send = kernel_call(
+        out_near_kernel, "out_near", pair_outs, places, near_attended, out_full
+    )
+    token_rows = kernel_call(
+        turn_kernel, "turn", [((SEQ, feats), BF)] * 4, places, *after(x_blocks, near_own)
+    )
+    near_got = flip(near_send, "dp")
+    got = after(got, near_got, token_rows)
+    chunk = own_rows // 2
+    row_chunk = stepped((chunk, width), 0)
+    own_tokens = pl.BlockSpec((feats, chunk), lambda step, places: (0, 2 * places[0] + step))
+    normed_a, low_a, normed1, scale1 = kernel_call(
+        norm1_kernel,
+        "norm1",
+        [(row_block, F32), (row_block, BF), (row_block, F32), ((own_rows, 1), F32)],
+        places,
+        near_own,
+        near_got,
+        got,
+        *x_blocks,
+        vec,
+        grid=2,
+        specs=[row_chunk] * 3 + [own_tokens] * 4 + [fixed((8, width))],
+        out_specs=[row_chunk] * 3 + [stepped((chunk, 1), 0)],
+    )
+
+    def up(rows_in):
+        pre = against(rows_in, up_full) + bias_up
+        cdf = 0.5 * (1.0 + lax.erf(pre * (0.5**0.5)))
+        slope = cdf + pre * (jnp.exp(-0.5 * pre * pre) * 0.3989422804014327)
+        return (pre * cdf).astype(BF), slope
+
+    a0, a1, a2 = low_a, flip(low_a, "dp"), flip(low_a, "t")
+    hidden_near, slope_near = up(jnp.concatenate([a0, a1]))
+    a2 = after(a2, hidden_near)
+    a3 = flip(a2, "dp")
+    hidden_far, slope_far = up(jnp.concatenate([a2, a3]))
+    far_send = matmul(hidden_far[own_rows:], down_full).astype(BF)
+    sent = to_far_chip(matmul(hidden_far[:own_rows], down_full), far_send)
+    near_hidden = after(hidden_near, sent)
+    got = flip(sent, "t")
+    near_got = flip(matmul(near_hidden[own_rows:], down_full).astype(BF), "dp")
+    near_own = matmul(near_hidden[:own_rows], down_full)
+    got = after(got, near_got)
+    turned_chunk = stepped((feats, chunk), 1)
+    pair_chunk = stepped((2, feats, chunk), 2)
+    result_here, result_send, grad_r2, low_g, sums2 = kernel_call(
+        norm2_kernel,
+        "norm2",
+        [((2, feats, own_rows), BF)] * 2 + [(row_block, F32), (row_block, BF), ((8, width), F32)],
+        places,
+        near_own,
+        near_got,
+        got,
+        normed_a,
+        cot_parts[0],
+        cot_far[0],
+        cot_near[0],
+        cot_near[1],
+        vec,
+        grid=2,
+        specs=[row_chunk] * 4 + [turned_chunk] * 4 + [fixed((8, width))],
+        out_specs=[pair_chunk] * 2 + [row_chunk] * 2 + [fixed((8, width))],
+    )
+
+    two_blocks = 2 * own_rows
+
+    def weight_grad(near, far, blocks, extra):
+        shape = (rows, ff_rows + extra, half)
+        return kernel_call(
+            weight_grad_kernel,
+            "weight_grad",
+            [(shape, BF)] * 2,
+            places,
+            near,
+            far,
+            *blocks,
+            grid=rows,
+            specs=[stepped((two_blocks, ff_rows), 1)] * 2 + [fixed(row_block)] * 4,
+            out_specs=[stepped((1, *shape[1:]), 0)] * 2,
+            scratch=[pltpu.VMEM((2, SEQ, half), BF)],
+        )
+
+    g0, g1, g2 = low_g, flip(low_g, "dp"), flip(low_g, "t")
+    grad_pre_near = (against(jnp.concatenate([g0, g1]), down_full) * slope_near).astype(BF)
+    g2 = after(g2, grad_pre_near)
+    g3 = flip(g2, "dp")
+    grad_pre_far = (against(jnp.concatenate([g2, g3]), down_full) * slope_far).astype(BF)
+    far_send = matmul(grad_pre_far[own_rows:], up_full).astype(BF)
+    sent = to_far_chip(matmul(grad_pre_far[:own_rows], up_full), far_send)
+    near_pre = after(grad_pre_near, sent)
+    got = flip(sent, "t")
+    near_got = flip(matmul(near_pre[own_rows:], up_full).astype(BF), "dp")
+    near_own = matmul(near_pre[:own_rows], up_full)
+    hiddens, pres = after(((hidden_near, hidden_far), (near_pre, grad_pre_far)), near_own)
+    down_mine, down_sent = weight_grad(*hiddens, (g0, g1, g2, g3), 0)
+    down_got = flip(down_sent, "u")
+    up_mine, up_sent = weight_grad(*pres, (a0, a1, a2, a3), 8)
+    got = after(got, near_got, up_sent)
+    low_r1, sums = kernel_call(
+        norm1_back_kernel,
+        "norm1_back",
+        [(row_block, BF), ((8, width), F32)],
+        places,
+        near_own,
+        near_got,
+        got,
+        grad_r2,
+        normed1,
+        scale1,
+        vec,
+        sums2,
+        grid=2,
+        specs=[row_chunk] * 5 + [stepped((chunk, 1), 0)] + [fixed((8, width))] * 2,
+        out_specs=[row_chunk, fixed((8, width))],
+    )
+
+    d0, d1, d2 = low_r1, flip(low_r1, "dp"), flip(low_r1, "t")
+    down_got = after(down_got, low_r1)
+    up_sent, down_got = lax.optimization_barrier((up_sent, down_got))
+    up_got = flip(up_sent, "u")
+    d2 = after(d2, down_got)
+    down_total = reduce_blocks(down_mine.astype(F32) + down_got.astype(F32))
+    d3 = flip(d2, "dp")
+    d_blocks = (d0, d1, d2, d3)
+    out_shape = (rows, 2, out_rows, feats)
+    grad_att, out_mine, out_sent = kernel_call(
+        out_back_kernel,
+        "out_back",
+        [((rows, head_rows, SEQ), BF)] + [(out_shape, BF)] * 2,
+        places,
+        *d_blocks,
+        out_full,
+        low_attended,
+    )
+    out_got = flip(out_sent, "u")
+    extra_rows = qkv_rows + 16
+    pair_of_heads = rows // 2
+
+    def attend_back(first, grad):
+        def of(shape):
+            return pl.BlockSpec(
+                shape, lambda step, places: (first + step,) + (0,) * (len(shape) - 1)
+            )
+
+        return kernel_call(
+            attend_back_kernel,
+            "attend_back",
+            [((pair_of_heads, qkv_rows, SEQ), BF)]
+            + [((pair_of_heads, 2, extra_rows, feats), BF)] * 2,
+            places,
+            qkv,
+            grad,
+            log_norm,
+            attended,
+            *token_rows,
+            sums,
+            grid=pair_of_heads,
+            specs=[
+                of((1, 3, head_rows, SEQ)),
+                of((1, head_rows, SEQ)),
+                of((1, 1, SEQ)),
+                of((1, head_rows, SEQ)),
+            ]
+            + [fixed((SEQ, feats))] * 4
+            + [fixed((8, width))],
+            out_specs=[stepped((1, qkv_rows, SEQ), 0)]
+            + [stepped((1, 2, extra_rows, feats), 0)] * 2,
+            scratch=[pltpu.VMEM((SEQ, SEQ), BF)] * 2,
+            vmem=30,
+        )
+
+    grads_late, late_mine, late_sent = attend_back(pair_of_heads, grad_att)
+    late_got = flip(late_sent, "u")
+    up_got = after(up_got, late_sent)
+    up_both = (up_mine.astype(F32) + up_got.astype(F32)).astype(BF)
+    grad_att, up_both = lax.optimization_barrier((grad_att, up_both))
+    up_total = reduce_blocks(up_both)
+    grads_early, early_mine, early_sent = attend_back(0, grad_att)
+    early_got = flip(early_sent, "u")
+    late_got = after(late_got, early_sent)
+    sum_shape = (2, extra_rows + out_rows, feats)
+    late_sums = kernel_call(
+        late_sum_kernel,
+        "late_sum",
+        [(sum_shape, BF)] * (rows - pair_of_heads),
+        places,
+        late_mine,
+        late_got,
+        out_mine,
+        out_got,
+    )
+    late_sums, grads_late = lax.optimization_barrier((late_sums, grads_late))
+    moved = [
+        shift(late_sums[i], "row", -(pair_of_heads + i)) for i in range(rows - pair_of_heads)
+    ]
+
+    grad_proj = jnp.concatenate([grads_early, grads_late])
+
+    def back_to(index):
+        return inner_rows(
+            weight[index].reshape(rows * qkv_rows, feats), grad_proj.reshape(rows * qkv_rows, SEQ)
+        )
+
+    sent = to_far_chip(back_to(1), back_to(3).astype(BF))
+    got = flip(sent, "t")
+    early_got = after(early_got, sent)
+    early_own, *early_sums = kernel_call(
+        early_sum_kernel,
+        "early_sum",
+        [(sum_shape, F32)] + [(sum_shape, BF)] * (pair_of_heads - 1),
+        places,
+        early_mine,
+        early_got,
+        out_mine,
+        out_got,
+    )
+    moved += [shift(early_sums[i - 1], "row", -i) for i in range(1, pair_of_heads)]
+    near_own, near_send = kernel_call(
+        input_near_kernel,
+        "input_near",
+        [((feats, SEQ), F32), ((feats, SEQ), BF)],
+        places,
+        *after((weight[0], weight[2]), sent),
+        grad_proj,
+        *d_blocks,
+        vmem=24,
+    )
+    grad_in = (near_own + flip(near_send, "dp").astype(F32) + got.astype(F32)).astype(BF)
+    grad_tokens = lax.ppermute(grad_in, ("dp", "u"), swap_cores)
+
+    def by_chip(total):
+        return cut(total, chip, feats, 1), cut(total, 1 - chip, feats, 1)
+
+    down_parts = spread_weights(*by_chip(after(down_total, sent)))
+    (down_out,) = kernel_call(
+        last_down_kernel, "last_down", [((4 * ff_rows, feats), F32)], places, *down_parts
+    )
+    up_parts = spread_weights(*by_chip(after(up_total, near_own)))
+    up_out, up_bias_out = kernel_call(
+        last_up_kernel,
+        "last_up",
+        [((feats, 4 * ff_rows), F32), ((1, 4 * ff_rows), F32)],
+        places,
+        *up_parts,
+    )
+    moved[-1] = after(moved[-1], down_out, up_out, grad_in)
+    qkv_sums = kernel_call(
+        last_sum_kernel,
+        "last_sum",
+        [((extra_rows + out_rows, feats), BF)] * 2,
+        places,
+        early_own,
+        *moved,
+    )
+    qkv_parts = spread_weights(*qkv_sums)
+    grad_tokens = after(grad_tokens, qkv_parts[2]).astype(F32)
+    qkv_out, qv_out, norm_out, out_out = kernel_call(
+        last_attn_kernel,
+        "last_attn",
+        [
+            ((3, feats, 4 * head_rows), F32),
+            ((2, 4 * head_rows), F32),
+            ((8, feats), F32),
+            ((4 * out_rows, feats), F32),
+        ],
+        places,
+        *qkv_parts,
+        scratch=[pltpu.VMEM((4 * head_rows, feats), F32)],
+    )
+
+    result_far = after(flip(after(result_send, grad_att), "t"), late_sent)
+    result_near = flip(jnp.stack([result_here[1], result_far[1]]), "dp")
+    result_parts = [result_here[0], result_near[0], result_far[0], result_near[1]]
+    result_seq = after(four_in_order(core, chip, result_parts, 1), early_sent)
+    result_out = lax.ppermute(result_seq, ("dp", "u"), swap_cores)
+    return (
+        result_out,
+        grad_tokens,
+        qkv_out.transpose(1, 0, 2),
+        qv_out,
+        out_out,
+        norm_out[0],
+        norm_out[1],
+        norm_out[2],
+        up_out,
+        up_bias_out[0],
+        down_out,
+        norm_out[3],
+        norm_out[4],
+        norm_out[5],
+    )
+
+
 def solution(mesh):
-    placed = (
-        P("col", ("dp", "row")),
-        P("col", None, "row"),
-        P(None, "row"),
-        P("row", "col"),
-        P("col"),
-        P("col"),
-        P("col"),
-        P("col", "row"),
-        P("row"),
-        P("row", "col"),
-        P("col"),
-        P("col"),
-        P("col"),
-        P("col", ("dp", "row")),
-    )
+    sizes = dict(mesh.shape)
+    grouped = sizes["dp"] == 2 and sizes["col"] == 4 and D % (4 * sizes["row"] * HEAD_DIM) == 0
+    if grouped:
+        devices = mesh.devices.reshape(sizes["dp"], sizes["row"], 2, 2)
+        inner_mesh, col, body = Mesh(devices, ("dp", "row", "u", "t")), ("u", "t"), fast_shards
+    else:
+        inner_mesh, col, body = mesh, "col", shards
+    tokens_spec = P(col, ("dp", "row"))
     return jax.shard_map(
-        shards,
-        mesh=mesh,
-        in_specs=placed,
+        body,
+        mesh=inner_mesh,
+        in_specs=(
+            tokens_spec,
+            P(col, None, "row"),
+            P(None, "row"),
+            P("row", col),
+            P(col),
+            P(col),
+            P(col),
+            P(col, "row"),
+            P("row"),
+            P("row", col),
+            P(col),
+            P(col),
+            P(col),
+            tokens_spec,
+        ),
         out_specs=(
-            P("col", ("dp", "row")),
-            P("col", ("dp", "row")),
-            P("col", None, "row"),
+            tokens_spec,
+            tokens_spec,
+            P(col, None, "row"),
             P(None, "row"),
-            P("row", "col"),
-            P("col"),
-            P("col"),
-            P("col"),
-            P("col", "row"),
+            P("row", col),
+            P(col),
+            P(col),
+            P(col),
+            P(col, "row"),
             P("row"),
-            P("row", "col"),
-            P("col"),
-            P("col"),
-            P("col"),
+            P("row", col),
+            P(col),
+            P(col),
+            P(col),
         ),
         check_vma=False,
     )

time: 1500 us -> 378 us (0.25)
  waiting for transfers between devices: 1220 us -> 152 us
  matrix products: 103 us -> 22.1 us
  Pallas kernels: 0 us -> 68.2 us
  starting transfers between devices: 1.81 us -> 65.8 us
  blocking collectives: 54.9 us -> 0 us
  other arithmetic: 65.5 us -> 13.9 us
    reduce_scatter x8 -> x2, waiting for transfers between devices: 725 us -> 0.01 us  [reduce_blocks(): return lax.psum_scatter(both.astype(BF), 'row', scatter_dimension=0)]
    all_gather x8 -> x2, waiting for transfers between devices: 471 us -> 12.9 us  [gather_blocks(): return lax.all_gather(payload, 'row', axis=0)]
    ppermute x0 -> x55, waiting for transfers between devices: none -> 139 us  [the longest x45 96.9 us: flip(): return lax.ppermute(values, axis_name, PAIR)]
    pallas_call x0 -> x21, Pallas kernels: none -> 68.2 us  [kernel_call(): pl.pallas_call(kernel, grid_spec=pltpu.PrefetchScalarGridSpec(num_scalar_...]
    ppermute x0 -> x55, starting transfers between devices: none -> 65.6 us  [the longest x45 46.8 us: flip(): return lax.ppermute(values, axis_name, PAIR)]
    psum x6 -> x0, blocking collectives: 54.9 us -> none  [the longest x4 31.5 us: feature_totals(): lax.psum((jnp.sum(first_terms, axis=1), jnp.sum(second_terms, axis=1)), '...]
    reduce_sum x11 -> x0, other arithmetic: 27.5 us -> none  [the longest x2 5.4 us: norm_backward(): jnp.sum(grad_in * normed, axis=0)]
    dot_general x12 -> x0, matrix products: 27.4 us -> none  [the longest x2 9.13 us: attention_backward(): jnp.einsum('nqhd,nkhd->nhqk', grad_block, value_seq, preferred_element_ty...]
  transfers between devices with their start and end apart: 17 -> 59, of which waited for: 17 -> 30; matrix products, arithmetic and copies ran while one was open for 2% -> 9% of each run, Pallas kernels for 0% -> 15%
where the time goes in v2:
time: 378 us; the launch traced here: 377 us
  waiting for transfers between devices  152 us (40%)
  Pallas kernels  68.2 us (18%)
  starting transfers between devices  65.8 us (17%)
  local copies, waits for them, and re-layouts  40.4 us (11%)
  matrix products  22.1 us (6%)
  between operations  14.9 us (4%)
  other arithmetic  13.9 us (4%)
    ppermute x45, waiting for transfers between devices, flip(): return lax.ppermute(values, axis_name, PAIR)  96.9 us
    pallas_call x21, Pallas kernels, kernel_call(): pl.pallas_call(kernel, grid_spec=pltpu.PrefetchScalarGridSpec(num_scalar_...  68.2 us
    ppermute x45, starting transfers between devices, flip(): return lax.ppermute(values, axis_name, PAIR)  46.8 us
    ppermute x6, waiting for transfers between devices, shift(): lax.ppermute(values, axis_name, [(i, (i + step) % size) for i in range(si...  31.6 us
    unnamed x204, local copies, waits for them, and re-layouts  31.3 us
    all_gather x2, waiting for transfers between devices, gather_blocks(): return lax.all_gather(payload, 'row', axis=0)  12.9 us
    dot_general x4, matrix products, against(): lax.dot_general(first_mat, second_mat, (((1,), (1,)), ((), ())), preferre...  10.7 us
  transfers between devices with their start and end apart: 59, of which 30 were waited for; matrix products, arithmetic and copies ran while one was open for 9% of the time, Pallas kernels for 15%

profile of v2, /device:TPU:1, one launch (start us, length us, event | category | flops | bytes accessed | tf_op | source)
XLA Modules:
  0.0 377.1 jit_solution(1040868821068148586)
XLA Ops:
  7.2 4.5 %collective-permute-start = (bf16[256,1024]{1,0:T(8,128)(2,1)}, bf16[256,1024]{1,0:T(8,128)(2,1)S(1)}, u32[]{:S(2)}, u32[]{:S(2)}) collective-permute-start(bf16[256,1024]{1,0:T(8,128)(2,1)} %param.14), channel_id=1, source_target_pairs={{0,0},{2,16},{16,2},{18,18},{1,1},{3,17},{17,3},{19,19},{4,4},{6,2... | collective-permute-start | bytes 1572872 | tf_op jit(solution)/shard_map/ppermute | solution.py:683
  12.4 2.7 prepare_attn.1
  16.3 2.7 prepare_ff.1
  21.7 4.9 %collective-permute-done.5 = bf16[512,256]{1,0:T(8,128)(2,1)S(1)} collective-permute-done((bf16[512,256]{1,0:T(8,128)(2,1)}, bf16[512,256]{1,0:T(8,128)(2,1)S(1)}, u32[]{:S(2)}, u32[]{:S(2)}) %collective-permute-start.5) | collective-permute-done | bytes 262176 | tf_op jit(solution)/shard_map/ppermute | solution.py:268
  28.5 3.4 collective-permute-start.8
  32.3 3.1 collective-permute-start.11
  36.6 20.9 %collective-permute-done.7 = bf16[2,200,256]{2,1,0:T(8,128)(2,1)S(1)} collective-permute-done((bf16[2,200,256]{2,1,0:T(8,128)(2,1)S(1)}, bf16[2,200,256]{2,1,0:T(8,128)(2,1)S(1)}, u32[]{:S(2)}, u32[]{:S(2)}) %collective-permute-start.7) | collective-permute-done | bytes 204832 | tf_op jit(solution)/shard_map/ppermute | solution.py:273
  61.5 4.5 %collective-permute-done.12 = bf16[2,256,256]{2,1,0:T(8,128)(2,1)S(1)} collective-permute-done((bf16[2,256,256]{2,1,0:T(8,128)(2,1)S(1)}, bf16[2,256,256]{2,1,0:T(8,128)(2,1)S(1)}, u32[]{:S(2)}, u32[]{:S(2)}) %collective-permute-start.12) | collective-permute-done | bytes 262176 | tf_op jit(solution)/shard_map/ppermute | solution.py:268
  66.7 4.7 %collective-permute-start.13 = (bf16[2,256,256]{2,1,0:T(8,128)(2,1)S(1)}, bf16[2,256,256]{2,1,0:T(8,128)(2,1)S(1)}, u32[]{:S(2)}, u32[]{:S(2)}) collective-permute-start(bf16[2,256,256]{2,1,0:T(8,128)(2,1)S(1)} %pad_maximum_fusion.7), channel_id=1, source_target_pairs={{0,16},{16,0},{1,17},{17,1},{2,18},{18,2},{3,19},{19,3},{4,20},{20... | collective-permute-start | bytes 786440 | tf_op jit(solution)/shard_map/ppermute | solution.py:268
  72.5 4.2 %collective-permute-done.10.far = bf16[4,2,200,256]{3,2,1,0:T(8,128)(2,1)S(1)} collective-permute-done((bf16[4,2,200,256]{3,2,1,0:T(8,128)(2,1)S(1)}, bf16[4,2,200,256]{3,2,1,0:T(8,128)(2,1)S(1)}, u32[]{:S(2)}, u32[]{:S(2)}) %collective-permute-start.10) | collective-permute-done | bytes 819232 | tf_op jit(solution)/shard_map/ppermute | solution.py:268
  84.7 14.3 %attend.1 = (bf16[4,3,64,1024]{3,2,1,0:T(8,128)(2,1)S(1)}, f32[4,64,1024]{2,1,0:T(8,128)S(1)}, f32[4,1,1024]{2,1,0:T(1,128)S(1)}, bf16[4,192,256]{2,1,0:T(8,128)...) custom-call(s32[6]{0:T(128)S(1)} %copy-done.75, ...), custom_call_target="tpu_custom_call" | custom-call | flops 1 | bytes 1 | tf_op jit(solution)/shard_map/attend/pallas_call | solution.py:301
  100.3 1.8 out_far.1
  104.6 6.0 %collective-permute-start.15 = (bf16[256,1024]{1,0:T(8,128)(2,1)}, bf16[256,1024]{1,0:T(8,128)(2,1)}, u32[]{:S(2)}, u32[]{:S(2)}) collective-permute-start(bf16[256,1024]{1,0:T(8,128)(2,1)} %get-tuple-element.134), channel_id=1, source_target_pairs={{0,16},{16,0},{1,17},{17,1},{2,18},{18,2},{3,19},{19,3},{4,20},{20... | collective-permute-start | bytes 1572872 | tf_op jit(solution)/shard_map/ppermute | solution.py:268
  118.7 8.2 %collective-permute-done.17.got = bf16[256,1024]{1,0:T(8,128)(2,1)S(1)} collective-permute-done((bf16[256,1024]{1,0:T(8,128)(2,1)S(1)}, bf16[256,1024]{1,0:T(8,128)(2,1)S(1)}, u32[]{:S(2)}, u32[]{:S(2)}) %collective-permute-start.17) | collective-permute-done | bytes 524320 | tf_op jit(solution)/shard_map/ppermute | solution.py:268
  126.8 1.8 norm1.1
  132.2 3.5 collective-permute-done.19
  135.9 2.7 multiply_convert_fusion.1
  138.7 5.8 %collective-permute-done.20.r2 = bf16[256,1024]{1,0:T(8,128)(2,1)S(1)} collective-permute-done((bf16[256,1024]{1,0:T(8,128)(2,1)S(1)}, bf16[256,1024]{1,0:T(8,128)(2,1)S(1)}, u32[]{:S(2)}, u32[]{:S(2)}) %collective-permute-start.20) | collective-permute-done | bytes 524320 | tf_op jit(solution)/shard_map/ppermute | solution.py:268
  146.7 2.7 multiply_convert_fusion
  151.1 12.9 %all-gather.7.cloned.1.call-done = bf16[1024,1024]{1,0:T(8,128)(2,1)} async-done(((bf16[256,1024]{1,0:T(8,128)(2,1)}), bf16[1024,1024]{1,0:T(8,128)(2,1)}) %all-gather.7.cloned.1.call-update) | async-done | bytes 2097168 | tf_op jit(solution)/shard_map/all_gather | solution.py:640
  164.0 2.4 convolution_convert_fusion.3
  173.7 8.9 %collective-permute-done.24.got = bf16[256,1024]{1,0:T(8,128)(2,1)S(1)} collective-permute-done((bf16[256,1024]{1,0:T(8,128)(2,1)S(1)}, bf16[256,1024]{1,0:T(8,128)(2,1)S(1)}, u32[]{:S(2)}, u32[]{:S(2)}) %collective-permute-start.24) | collective-permute-done | bytes 524320 | tf_op jit(solution)/shard_map/ppermute | solution.py:268
  182.7 2.5 norm2.1
  188.7 2.6 fusion.5.left_near
  191.3 9.4 %collective-permute-done.26.r2 = bf16[256,1024]{1,0:T(8,128)(2,1)S(1)} collective-permute-done((bf16[256,1024]{1,0:T(8,128)(2,1)S(1)}, bf16[256,1024]{1,0:T(8,128)(2,1)S(1)}, u32[]{:S(2)}, u32[]{:S(2)}) %collective-permute-start.26) | collective-permute-done | bytes 524320 | tf_op jit(solution)/shard_map/ppermute | solution.py:268
  203.0 2.6 fusion.11.left_far
  209.8 4.0 %weight_grad.3 = (bf16[4,256,512]{2,1,0:T(8,128)(2,1)S(1)}, bf16[4,256,512]{2,1,0:T(8,128)(2,1)S(1)}) custom-call(s32[6]{0:T(128)S(1)} %copy-done.75, bf16[512,1024]{1,0:T(8,128)(2,1)S(1)} %get-tuple-element.168.left_near, bf16[512,1024]{1,0:T(8,128)(2,1)S(1)} %get-tuple-element.169.left_far, bf16[256,1024]{1,0:T(8,128)(2,1)S(1)} %get-tuple-element.156.r0, ...), custom_call_target="tpu_custom_call" | custom-call | flops 1 | bytes 1 | tf_op jit(solution)/shard_map/weight_grad/pallas_call | solution.py:301
  217.7 4.0 %weight_grad.2 = (bf16[4,264,512]{2,1,0:T(8,128)(2,1)S(1)}, bf16[4,264,512]{2,1,0:T(8,128)(2,1)S(1)}) custom-call(s32[6]{0:T(128)S(1)} %copy-done.75, bf16[512,1024]{1,0:T(8,128)(2,1)S(1)} %fusion.5.left_near, bf16[512,1024]{1,0:T(8,128)(2,1)S(1)} %fusion.11.left_far, bf16[256,1024]{1,0:T(8,128)(2,1)S(1)} %copy-done.55, bf16[256,1024]{1,0:T(8,128)(2,1)S(1)} %copy-done.57, ...), custom_call_target="tpu_custom_call" | custom-call | flops 1 | bytes 1 | tf_op jit(solution)/shard_map/weight_grad/pallas_call | solution.py:301
  222.8 7.3 %collective-permute-done.30.got = bf16[256,1024]{1,0:T(8,128)(2,1)S(1)} collective-permute-done((bf16[256,1024]{1,0:T(8,128)(2,1)S(1)}, bf16[256,1024]{1,0:T(8,128)(2,1)S(1)}, u32[]{:S(2)}, u32[]{:S(2)}) %collective-permute-start.30) | collective-permute-done | bytes 524320 | tf_op jit(solution)/shard_map/ppermute | solution.py:268
  231.6 6.7 %collective-permute-done.33 = bf16[4,256,512]{2,1,0:T(8,128)(2,1)S(1)} collective-permute-done((bf16[4,256,512]{2,1,0:T(8,128)(2,1)S(1)}, bf16[4,256,512]{2,1,0:T(8,128)(2,1)S(1)}, u32[]{:S(2)}, u32[]{:S(2)}) %collective-permute-start.33) | collective-permute-done | bytes 1048608 | tf_op jit(solution)/shard_map/ppermute | solution.py:268
  242.1 1.8 collective-permute-start.31
  243.8 9.1 %collective-permute-done.32.d2 = bf16[256,1024]{1,0:T(8,128)(2,1)S(1)} collective-permute-done((bf16[256,1024]{1,0:T(8,128)(2,1)S(1)}, bf16[256,1024]{1,0:T(8,128)(2,1)S(1)}, u32[]{:S(2)}, u32[]{:S(2)}) %collective-permute-start.32) | collective-permute-done | bytes 524320 | tf_op jit(solution)/shard_map/ppermute | solution.py:268
  252.9 2.3 collective-permute-start.34
  256.8 1.9 out_back.1
  265.2 9.5 %attend_back.2 = (bf16[2,192,1024]{2,1,0:T(8,128)(2,1)S(1)}, bf16[2,2,208,256]{3,2,1,0:T(8,128)(2,1)S(1)}, bf16[2,2,208,256]{3,2,1,0:T(8,128)(2,1)S(1)}) custom-call(s32[6]{0:T(128)S(1)} %copy-done.75, bf16[4,3,64,1024]{3,2,1,0:T(8,128)(2,1)S(1)} %copy-done.2, bf16[4,64,1024]{2,1,0:T(8,128)(2,1)S(1)} %get-tuple-element.182.grad_ref, ...), custom_call_target="tpu_custom_call" | custom-call | flops 1 | bytes 1 | tf_op jit(solution)/shard_map/attend_back/pallas_call | solution.py:301
  284.6 9.3 %attend_back.3 = (bf16[2,192,1024]{2,1,0:T(8,128)(2,1)S(1)}, bf16[2,2,208,256]{3,2,1,0:T(8,128)(2,1)S(1)}, bf16[2,2,208,256]{3,2,1,0:T(8,128)(2,1)S(1)}) custom-call(s32[6]{0:T(128)S(1)} %copy-done.75, bf16[4,3,64,1024]{3,2,1,0:T(8,128)(2,1)S(1)} %copy-done.3, bf16[4,64,1024]{2,1,0:T(8,128)(2,1)S(1)} %copy-done.35, ...), custom_call_target="tpu_custom_call" | custom-call | flops 1 | bytes 1 | tf_op jit(solution)/shard_map/attend_back/pallas_call | solution.py:301
  300.7 6.4 %collective-permute-done.36 = bf16[2,256,256]{2,1,0:T(8,128)(2,1)} collective-permute-done((bf16[2,256,256]{2,1,0:T(8,128)(2,1)S(1)}, bf16[2,256,256]{2,1,0:T(8,128)(2,1)}, u32[]{:S(2)}, u32[]{:S(2)}) %collective-permute-start.36) | collective-permute-done | bytes 262176 | tf_op jit(solution)/shard_map/ppermute | solution.py:268
  309.8 2.5 fusion.13
  313.5 1.9 input_near.1
  324.8 3.9 %collective-permute-done.49.p2 = bf16[256,256]{1,0:T(8,128)(2,1)S(1)} collective-permute-done((bf16[256,256]{1,0:T(8,128)(2,1)}, bf16[256,256]{1,0:T(8,128)(2,1)S(1)}, u32[]{:S(2)}, u32[]{:S(2)}) %collective-permute-start.49) | collective-permute-done | bytes 131104 | tf_op jit(solution)/shard_map/ppermute | solution.py:268
  328.7 2.9 collective-permute-done.51.p2
  332.5 1.7 collective-permute-start.50
  339.1 9.9 %collective-permute-done.48.refs_2_ = bf16[2,272,256]{2,1,0:T(8,128)(2,1)S(1)} collective-permute-done((bf16[2,272,256]{2,1,0:T(8,128)(2,1)S(1)}, bf16[2,272,256]{2,1,0:T(8,128)(2,1)S(1)}, u32[]{:S(2)}, u32[]{:S(2)}) %collective-permute-start.48) | collective-permute-done | bytes 278560 | tf_op jit(solution)/shard_map/ppermute | solution.py:273
  350.2 2.8 collective-permute-start.38
  353.0 2.7 collective-permute-start.44
  356.0 4.7 %collective-permute-done.38 = bf16[256,1024]{1,0:T(8,128)(2,1)S(1)} collective-permute-done((bf16[256,1024]{1,0:T(8,128)(2,1)S(1)}, bf16[256,1024]{1,0:T(8,128)(2,1)S(1)}, u32[]{:S(2)}, u32[]{:S(2)}) %collective-permute-start.38) | collective-permute-done | bytes 524320 | tf_op jit(solution)/shard_map/ppermute | solution.py:1054
  360.7 5.6 %collective-permute-done.44 = bf16[256,1024]{1,0:T(8,128)(2,1)S(1)} collective-permute-done((bf16[256,1024]{1,0:T(8,128)(2,1)S(1)}, bf16[256,1024]{1,0:T(8,128)(2,1)S(1)}, u32[]{:S(2)}, u32[]{:S(2)}) %collective-permute-start.44) | collective-permute-done | bytes 524320 | tf_op jit(solution)/shard_map/ppermute | solution.py:1008
  367.4 1.8 last_attn.1
  (357 shorter events, 115.5 us)
Async XLA Ops:
  7.2 70.4 %all-gather.5.cloned.1.call-start = ((), (), s32[]{:S(2)}) async-start(), calls=%async_computation.4 | async-start | bytes 1720320 | tf_op jit(solution)/shard_map/all_gather | solution.py:640
  7.2 13.7 %collective-permute-start = (bf16[256,1024]{1,0:T(8,128)(2,1)}, bf16[256,1024]{1,0:T(8,128)(2,1)S(1)}, u32[]{:S(2)}, u32[]{:S(2)}) collective-permute-start(bf16[256,1024]{1,0:T(8,128)(2,1)} %param.14), channel_id=1, source_target_pairs={{0,0},{2,16},{16,2},{18,18},{1,1},{3,17},{17,3},{19,19},{4,4},{6,2... | collective-permute-start | bytes 1572872 | tf_op jit(solution)/shard_map/ppermute | solution.py:683
  19.0 7.6 %collective-permute-start.5 = (bf16[512,256]{1,0:T(8,128)(2,1)}, bf16[512,256]{1,0:T(8,128)(2,1)S(1)}, u32[]{:S(2)}, u32[]{:S(2)}) collective-permute-start(bf16[512,256]{1,0:T(8,128)(2,1)} %get-tuple-element.123), channel_id=1, source_target_pairs={{0,1},{1,0},{2,3},{3,2},{4,5},{5,4},{6,7},{7,6},{8,9},{9,8},{10,11... | collective-permute-start | bytes 786440 | tf_op jit(solution)/shard_map/ppermute | solution.py:268
  28.4 135.5 %all-gather.7.cloned.1.call-start = ((), (), s32[]{:S(2)}) async-start(), calls=%async_computation.5 | async-start | bytes 2621440 | tf_op jit(solution)/shard_map/all_gather | solution.py:640
  28.5 8.1 %collective-permute-start.8 = (bf16[2,200,256]{2,1,0:T(8,128)(2,1)S(1)}, bf16[2,200,256]{2,1,0:T(8,128)(2,1)S(1)}, u32[]{:S(2)}, u32[]{:S(2)}) collective-permute-start(bf16[2,200,256]{2,1,0:T(8,128)(2,1)S(1)} %pad_maximum_fusion.10), channel_id=1, source_target_pairs={{0,12},{4,0},{8,4},{12,8},{1,13},{5,1},{9,5},{13,9},{2,14},{6,2},{... | collective-permute-start | bytes 614408 | tf_op jit(solution)/shard_map/ppermute | solution.py:273
  31.9 25.6 %collective-permute-start.7 = (bf16[2,200,256]{2,1,0:T(8,128)(2,1)S(1)}, bf16[2,200,256]{2,1,0:T(8,128)(2,1)S(1)}, u32[]{:S(2)}, u32[]{:S(2)}) collective-permute-start(bf16[2,200,256]{2,1,0:T(8,128)(2,1)S(1)} %pad_maximum_fusion.10), channel_id=1, source_target_pairs={{0,8},{4,12},{8,0},{12,4},{1,9},{5,13},{9,1},{13,5},{2,10},{6,14},... | collective-permute-start | bytes 614408 | tf_op jit(solution)/shard_map/ppermute | solution.py:273
  31.9 25.6 %collective-permute-start.6 = (bf16[2,200,256]{2,1,0:T(8,128)(2,1)S(1)}, bf16[2,200,256]{2,1,0:T(8,128)(2,1)}, u32[]{:S(2)}, u32[]{:S(2)}) collective-permute-start(bf16[2,200,256]{2,1,0:T(8,128)(2,1)S(1)} %pad_maximum_fusion.10), channel_id=1, source_target_pairs={{0,4},{4,8},{8,12},{12,0},{1,5},{5,9},{9,13},{13,1},{2,6},{6,10},{... | collective-permute-start | bytes 614408 | tf_op jit(solution)/shard_map/ppermute | solution.py:273
  32.3 27.1 %collective-permute-start.11 = (bf16[256,1024]{1,0:T(8,128)(2,1)}, bf16[256,1024]{1,0:T(8,128)(2,1)S(1)}, u32[]{:S(2)}, u32[]{:S(2)}) collective-permute-start(bf16[256,1024]{1,0:T(8,128)(2,1)} %param.27), channel_id=1, source_target_pairs={{0,0},{2,16},{16,2},{18,18},{1,1},{3,17},{17,3},{19,19},{4,4},{6,2... | collective-permute-start | bytes 1572872 | tf_op jit(solution)/shard_map/ppermute | solution.py:709
  35.5 24.0 %collective-permute-start.1 = (bf16[256,1024]{1,0:T(8,128)(2,1)S(1)}, bf16[256,1024]{1,0:T(8,128)(2,1)S(1)}, u32[]{:S(2)}, u32[]{:S(2)}) collective-permute-start(bf16[256,1024]{1,0:T(8,128)(2,1)S(1)} %collective-permute-done.x00.refs_0_), channel_id=1, source_target_pairs={{0,1},{1,0},{2,3},{3,2},{4,5},{5,4},{6,7},{7,6},{8,9},{9,8},{10,11... | collective-permute-start | bytes 1572872 | tf_op jit(solution)/shard_map/ppermute | solution.py:268
  36.6 22.8 %collective-permute-start.9 = (bf16[256,512]{1,0:T(8,128)(2,1)S(1)}, bf16[256,512]{1,0:T(8,128)(2,1)S(1)}, u32[]{:S(2)}, u32[]{:S(2)}) collective-permute-start(bf16[256,512]{1,0:T(8,128)(2,1)S(1)} %fusion.48), channel_id=1, source_target_pairs={{0,2},{2,0},{1,3},{3,1},{4,6},{6,4},{5,7},{7,5},{8,10},{10,8},{9,1... | collective-permute-start | bytes 786440 | tf_op jit(solution)/shard_map/ppermute | solution.py:268
  61.5 15.2 %collective-permute-start.10 = (bf16[4,2,200,256]{3,2,1,0:T(8,128)(2,1)S(1)}, bf16[4,2,200,256]{3,2,1,0:T(8,128)(2,1)S(1)}, u32[]{:S(2)}, u32[]{:S(2)}) collective-permute-start(bf16[4,2,200,256]{3,2,1,0:T(8,128)(2,1)S(1)} %pad_maximum_fusion.1.own), channel_id=1, source_target_pairs={{0,2},{2,0},{1,3},{3,1},{4,6},{6,4},{5,7},{7,5},{8,10},{10,8},{9,1... | collective-permute-start | bytes 2457608 | tf_op jit(solution)/shard_map/ppermute | solution.py:268
  66.7 5.9 %collective-permute-start.13 = (bf16[2,256,256]{2,1,0:T(8,128)(2,1)S(1)}, bf16[2,256,256]{2,1,0:T(8,128)(2,1)S(1)}, u32[]{:S(2)}, u32[]{:S(2)}) collective-permute-start(bf16[2,256,256]{2,1,0:T(8,128)(2,1)S(1)} %pad_maximum_fusion.7), channel_id=1, source_target_pairs={{0,16},{16,0},{1,17},{17,1},{2,18},{18,2},{3,19},{19,3},{4,20},{20... | collective-permute-start | bytes 786440 | tf_op jit(solution)/shard_map/ppermute | solution.py:268
  71.4 7.4 %collective-permute-start.2 = (bf16[256,1024]{1,0:T(8,128)(2,1)S(1)}, bf16[256,1024]{1,0:T(8,128)(2,1)S(1)}, u32[]{:S(2)}, u32[]{:S(2)}) collective-permute-start(bf16[256,1024]{1,0:T(8,128)(2,1)S(1)} %collective-permute-done.x00.refs_0_), channel_id=1, source_target_pairs={{0,16},{16,0},{1,17},{17,1},{2,18},{18,2},{3,19},{19,3},{4,20},{20... | collective-permute-start | bytes 1572872 | tf_op jit(solution)/shard_map/ppermute | solution.py:268
  71.4 8.1 %collective-permute-start.3 = (bf16[256,1024]{1,0:T(8,128)(2,1)S(1)}, bf16[256,1024]{1,0:T(8,128)(2,1)S(1)}, u32[]{:S(2)}, u32[]{:S(2)}) collective-permute-start(bf16[256,1024]{1,0:T(8,128)(2,1)S(1)} %collective-permute-done.1.x01.refs_1_), channel_id=1, source_target_pairs={{0,16},{16,0},{1,17},{17,1},{2,18},{18,2},{3,19},{19,3},{4,20},{20... | collective-permute-start | bytes 1572872 | tf_op jit(solution)/shard_map/ppermute | solution.py:268
  78.7 21.6 %collective-permute-start.14 = (bf16[4,72,512]{2,1,0:T(8,128)(2,1)S(1)}, bf16[4,72,512]{2,1,0:T(8,128)(2,1)S(1)}, u32[]{:S(2)}, u32[]{:S(2)}) collective-permute-start(bf16[4,72,512]{2,1,0:T(8,128)(2,1)S(1)} %slice.131), channel_id=1, source_target_pairs={{0,2},{2,0},{1,3},{3,1},{4,6},{6,4},{5,7},{7,5},{8,10},{10,8},{9,1... | collective-permute-start | bytes 884744 | tf_op jit(solution)/shard_map/ppermute | solution.py:268
  104.6 7.8 %collective-permute-start.15 = (bf16[256,1024]{1,0:T(8,128)(2,1)}, bf16[256,1024]{1,0:T(8,128)(2,1)}, u32[]{:S(2)}, u32[]{:S(2)}) collective-permute-start(bf16[256,1024]{1,0:T(8,128)(2,1)} %get-tuple-element.134), channel_id=1, source_target_pairs={{0,16},{16,0},{1,17},{17,1},{2,18},{18,2},{3,19},{19,3},{4,20},{20... | collective-permute-start | bytes 1572872 | tf_op jit(solution)/shard_map/ppermute | solution.py:268
  110.6 206.3 %reduce-scatter.3.cloned.1.call-start = ((), (), s32[]{:S(2)}) async-start(), calls=%async_computation.2 | async-start | bytes 1310720 | tf_op jit(solution)/shard_map/reduce_scatter | solution.py:644
  110.8 24.9 %collective-permute-start.19 = (bf16[4,256,512]{2,1,0:T(8,128)(2,1)S(1)}, bf16[4,256,512]{2,1,0:T(8,128)(2,1)S(1)}, u32[]{:S(2)}, u32[]{:S(2)}) collective-permute-start(bf16[4,256,512]{2,1,0:T(8,128)(2,1)S(1)} %slice.134), channel_id=1, source_target_pairs={{0,2},{2,0},{1,3},{3,1},{4,6},{6,4},{5,7},{7,5},{8,10},{10,8},{9,1... | collective-permute-start | bytes 3145736 | tf_op jit(solution)/shard_map/ppermute | solution.py:268
  113.6 13.2 %collective-permute-start.17 = (bf16[256,1024]{1,0:T(8,128)(2,1)S(1)}, bf16[256,1024]{1,0:T(8,128)(2,1)S(1)}, u32[]{:S(2)}, u32[]{:S(2)}) collective-permute-start(bf16[256,1024]{1,0:T(8,128)(2,1)S(1)} %add_convert_fusion.3), channel_id=1, source_target_pairs={{0,1},{1,0},{2,3},{3,2},{4,5},{5,4},{6,7},{7,6},{8,9},{9,8},{10,11... | collective-permute-start | bytes 1572872 | tf_op jit(solution)/shard_map/ppermute | solution.py:268
  116.0 10.8 %collective-permute-start.16 = (bf16[256,1024]{1,0:T(8,128)(2,1)S(1)}, bf16[256,1024]{1,0:T(8,128)(2,1)S(1)}, u32[]{:S(2)}, u32[]{:S(2)}) collective-permute-start(bf16[256,1024]{1,0:T(8,128)(2,1)S(1)} %get-tuple-element.138), channel_id=1, source_target_pairs={{0,16},{16,0},{1,17},{17,1},{2,18},{18,2},{3,19},{19,3},{4,20},{20... | collective-permute-start | bytes 1572872 | tf_op jit(solution)/shard_map/ppermute | solution.py:268
  129.6 6.3 %collective-permute-start.18 = (bf16[256,1024]{1,0:T(8,128)(2,1)S(1)}, bf16[256,1024]{1,0:T(8,128)(2,1)S(1)}, u32[]{:S(2)}, u32[]{:S(2)}) collective-permute-start(bf16[256,1024]{1,0:T(8,128)(2,1)S(1)} %get-tuple-element.148.r0), channel_id=1, source_target_pairs={{0,16},{16,0},{1,17},{17,1},{2,18},{18,2},{3,19},{19,3},{4,20},{20... | collective-permute-start | bytes 1572872 | tf_op jit(solution)/shard_map/ppermute | solution.py:268
  130.8 13.6 %collective-permute-start.20 = (bf16[256,1024]{1,0:T(8,128)(2,1)S(1)}, bf16[256,1024]{1,0:T(8,128)(2,1)S(1)}, u32[]{:S(2)}, u32[]{:S(2)}) collective-permute-start(bf16[256,1024]{1,0:T(8,128)(2,1)S(1)} %get-tuple-element.148.r0), channel_id=1, source_target_pairs={{0,1},{1,0},{2,3},{3,2},{4,5},{5,4},{6,7},{7,6},{8,9},{9,8},{10,11... | collective-permute-start | bytes 1572872 | tf_op jit(solution)/shard_map/ppermute | solution.py:268
  169.5 13.2 %collective-permute-start.24 = (bf16[256,1024]{1,0:T(8,128)(2,1)S(1)}, bf16[256,1024]{1,0:T(8,128)(2,1)S(1)}, u32[]{:S(2)}, u32[]{:S(2)}) collective-permute-start(bf16[256,1024]{1,0:T(8,128)(2,1)S(1)} %fusion.15), channel_id=1, source_target_pairs={{0,1},{1,0},{2,3},{3,2},{4,5},{5,4},{6,7},{7,6},{8,9},{9,8},{10,11... | collective-permute-start | bytes 1572872 | tf_op jit(solution)/shard_map/ppermute | solution.py:268
  187.1 13.6 %collective-permute-start.26 = (bf16[256,1024]{1,0:T(8,128)(2,1)S(1)}, bf16[256,1024]{1,0:T(8,128)(2,1)S(1)}, u32[]{:S(2)}, u32[]{:S(2)}) collective-permute-start(bf16[256,1024]{1,0:T(8,128)(2,1)S(1)} %get-tuple-element.156.r0), channel_id=1, source_target_pairs={{0,1},{1,0},{2,3},{3,2},{4,5},{5,4},{6,7},{7,6},{8,9},{9,8},{10,11... | collective-permute-start | bytes 1572872 | tf_op jit(solution)/shard_map/ppermute | solution.py:268
  213.8 24.4 %collective-permute-start.33 = (bf16[4,256,512]{2,1,0:T(8,128)(2,1)S(1)}, bf16[4,256,512]{2,1,0:T(8,128)(2,1)S(1)}, u32[]{:S(2)}, u32[]{:S(2)}) collective-permute-start(bf16[4,256,512]{2,1,0:T(8,128)(2,1)S(1)} %get-tuple-element.170), channel_id=1, source_target_pairs={{0,2},{2,0},{1,3},{3,1},{4,6},{6,4},{5,7},{7,5},{8,10},{10,8},{9,1... | collective-permute-start | bytes 3145736 | tf_op jit(solution)/shard_map/ppermute | solution.py:268
  215.8 7.0 %collective-permute-start.29 = (bf16[256,1024]{1,0:T(8,128)(2,1)S(1)}, bf16[256,1024]{1,0:T(8,128)(2,1)S(1)}, u32[]{:S(2)}, u32[]{:S(2)}) collective-permute-start(bf16[256,1024]{1,0:T(8,128)(2,1)S(1)} %convolution_convert_fusion), channel_id=1, source_target_pairs={{0,16},{16,0},{1,17},{17,1},{2,18},{18,2},{3,19},{19,3},{4,20},{20... | collective-permute-start | bytes 1572872 | tf_op jit(solution)/shard_map/ppermute | solution.py:268
  216.5 13.5 %collective-permute-start.30 = (bf16[256,1024]{1,0:T(8,128)(2,1)S(1)}, bf16[256,1024]{1,0:T(8,128)(2,1)S(1)}, u32[]{:S(2)}, u32[]{:S(2)}) collective-permute-start(bf16[256,1024]{1,0:T(8,128)(2,1)S(1)} %fusion.16), channel_id=1, source_target_pairs={{0,1},{1,0},{2,3},{3,2},{4,5},{5,4},{6,7},{7,6},{8,9},{9,8},{10,11... | collective-permute-start | bytes 1572872 | tf_op jit(solution)/shard_map/ppermute | solution.py:268
  239.6 79.3 %reduce-scatter.5.cloned.1.call-start = ((), (), s32[]{:S(2)}) async-start(), calls=%async_computation.3 | async-start | bytes 1351680 | tf_op jit(solution)/shard_map/reduce_scatter | solution.py:644
  239.7 36.8 %collective-permute-start.35 = (bf16[4,264,512]{2,1,0:T(8,128)(2,1)}, bf16[4,264,512]{2,1,0:T(8,128)(2,1)S(1)}, u32[]{:S(2)}, u32[]{:S(2)}) collective-permute-start(bf16[4,264,512]{2,1,0:T(8,128)(2,1)} %copy-done.78), channel_id=1, source_target_pairs={{0,2},{2,0},{1,3},{3,1},{4,6},{6,4},{5,7},{7,5},{8,10},{10,8},{9,1... | collective-permute-start | bytes 3244040 | tf_op jit(solution)/shard_map/ppermute | solution.py:268
  240.9 12.0 %collective-permute-start.32 = (bf16[256,1024]{1,0:T(8,128)(2,1)S(1)}, bf16[256,1024]{1,0:T(8,128)(2,1)S(1)}, u32[]{:S(2)}, u32[]{:S(2)}) collective-permute-start(bf16[256,1024]{1,0:T(8,128)(2,1)S(1)} %get-tuple-element.167.d0), channel_id=1, source_target_pairs={{0,1},{1,0},{2,3},{3,2},{4,5},{5,4},{6,7},{7,6},{8,9},{9,8},{10,11... | collective-permute-start | bytes 1572872 | tf_op jit(solution)/shard_map/ppermute | solution.py:268
  242.1 13.2 %collective-permute-start.31 = (bf16[256,1024]{1,0:T(8,128)(2,1)S(1)}, bf16[256,1024]{1,0:T(8,128)(2,1)S(1)}, u32[]{:S(2)}, u32[]{:S(2)}) collective-permute-start(bf16[256,1024]{1,0:T(8,128)(2,1)S(1)} %get-tuple-element.167.d0), channel_id=1, source_target_pairs={{0,16},{16,0},{1,17},{17,1},{2,18},{18,2},{3,19},{19,3},{4,20},{20... | collective-permute-start | bytes 1572872 | tf_op jit(solution)/shard_map/ppermute | solution.py:268
  278.6 15.4 %collective-permute-start.39 = (bf16[2,2,208,256]{3,2,1,0:T(8,128)(2,1)}, bf16[2,2,208,256]{3,2,1,0:T(8,128)(2,1)S(1)}, u32[]{:S(2)}, u32[]{:S(2)}) collective-permute-start(bf16[2,2,208,256]{3,2,1,0:T(8,128)(2,1)} %copy-done.80), channel_id=1, source_target_pairs={{0,2},{2,0},{1,3},{3,1},{4,6},{6,4},{5,7},{7,5},{8,10},{10,8},{9,1... | collective-permute-start | bytes 1277960 | tf_op jit(solution)/shard_map/ppermute | solution.py:268
  278.9 16.7 %collective-permute-start.40 = (bf16[4,2,64,256]{3,2,1,0:T(8,128)(2,1)}, bf16[4,2,64,256]{3,2,1,0:T(8,128)(2,1)S(1)}, u32[]{:S(2)}, u32[]{:S(2)}) collective-permute-start(bf16[4,2,64,256]{3,2,1,0:T(8,128)(2,1)} %copy-done.90), channel_id=1, source_target_pairs={{0,2},{2,0},{1,3},{3,1},{4,6},{6,4},{5,7},{7,5},{8,10},{10,8},{9,1... | collective-permute-start | bytes 786440 | tf_op jit(solution)/shard_map/ppermute | solution.py:268
  298.1 11.7 %collective-permute-start.41 = (bf16[256,1024]{1,0:T(8,128)(2,1)}, bf16[256,1024]{1,0:T(8,128)(2,1)}, u32[]{:S(2)}, u32[]{:S(2)}) collective-permute-start(bf16[256,1024]{1,0:T(8,128)(2,1)} %fusion.14), channel_id=1, source_target_pairs={{0,16},{16,0},{1,17},{17,1},{2,18},{18,2},{3,19},{19,3},{4,20},{20... | collective-permute-start | bytes 1572872 | tf_op jit(solution)/shard_map/ppermute | solution.py:268
  299.2 8.0 %collective-permute-start.36 = (bf16[2,256,256]{2,1,0:T(8,128)(2,1)S(1)}, bf16[2,256,256]{2,1,0:T(8,128)(2,1)}, u32[]{:S(2)}, u32[]{:S(2)}) collective-permute-start(bf16[2,256,256]{2,1,0:T(8,128)(2,1)S(1)} %copy-done.89), channel_id=1, source_target_pairs={{0,1},{1,0},{2,3},{3,2},{4,5},{5,4},{6,7},{7,6},{8,9},{9,8},{10,11... | collective-permute-start | bytes 786440 | tf_op jit(solution)/shard_map/ppermute | solution.py:268
  300.4 21.9 %collective-permute-start.45 = (bf16[2,2,208,256]{3,2,1,0:T(8,128)(2,1)}, bf16[2,2,208,256]{3,2,1,0:T(8,128)(2,1)}, u32[]{:S(2)}, u32[]{:S(2)}) collective-permute-start(bf16[2,2,208,256]{3,2,1,0:T(8,128)(2,1)} %copy-done.79), channel_id=1, source_target_pairs={{0,2},{2,0},{1,3},{3,1},{4,6},{6,4},{5,7},{7,5},{8,10},{10,8},{9,1... | collective-permute-start | bytes 1277960 | tf_op jit(solution)/shard_map/ppermute | solution.py:268
  308.8 11.0 %collective-permute-start.37 = (bf16[2,256,256]{2,1,0:T(8,128)(2,1)}, bf16[2,256,256]{2,1,0:T(8,128)(2,1)}, u32[]{:S(2)}, u32[]{:S(2)}) collective-permute-start(bf16[2,256,256]{2,1,0:T(8,128)(2,1)} %pad_maximum_fusion.8), channel_id=1, source_target_pairs={{0,16},{16,0},{1,17},{17,1},{2,18},{18,2},{3,19},{19,3},{4,20},{20... | collective-permute-start | bytes 786440 | tf_op jit(solution)/shard_map/ppermute | solution.py:268
  312.3 21.9 %collective-permute-start.43 = (bf16[256,1024]{1,0:T(8,128)(2,1)}, bf16[256,1024]{1,0:T(8,128)(2,1)}, u32[]{:S(2)}, u32[]{:S(2)}) collective-permute-start(bf16[256,1024]{1,0:T(8,128)(2,1)} %fusion.13), channel_id=1, source_target_pairs={{0,1},{1,0},{2,3},{3,2},{4,5},{5,4},{6,7},{7,6},{8,9},{9,8},{10,11... | collective-permute-start | bytes 1572872 | tf_op jit(solution)/shard_map/ppermute | solution.py:268
  316.4 16.1 %collective-permute-start.42 = (bf16[256,1024]{1,0:T(8,128)(2,1)}, bf16[256,1024]{1,0:T(8,128)(2,1)}, u32[]{:S(2)}, u32[]{:S(2)}) collective-permute-start(bf16[256,1024]{1,0:T(8,128)(2,1)} %get-tuple-element.203), channel_id=1, source_target_pairs={{0,16},{16,0},{1,17},{17,1},{2,18},{18,2},{3,19},{19,3},{4,20},{20... | collective-permute-start | bytes 1572872 | tf_op jit(solution)/shard_map/ppermute | solution.py:268
  318.6 10.2 %collective-permute-start.49 = (bf16[256,256]{1,0:T(8,128)(2,1)}, bf16[256,256]{1,0:T(8,128)(2,1)S(1)}, u32[]{:S(2)}, u32[]{:S(2)}) collective-permute-start(bf16[256,256]{1,0:T(8,128)(2,1)} %get-tuple-element.250), channel_id=1, source_target_pairs={{0,1},{1,0},{2,3},{3,2},{4,5},{5,4},{6,7},{7,6},{8,9},{9,8},{10,11... | collective-permute-start | bytes 393224 | tf_op jit(solution)/shard_map/ppermute | solution.py:268
  319.9 11.7 %collective-permute-start.51 = (bf16[264,256]{1,0:T(8,128)(2,1)S(1)}, bf16[264,256]{1,0:T(8,128)(2,1)S(1)}, u32[]{:S(2)}, u32[]{:S(2)}) collective-permute-start(bf16[264,256]{1,0:T(8,128)(2,1)S(1)} %get-tuple-element.246), channel_id=1, source_target_pairs={{0,1},{1,0},{2,3},{3,2},{4,5},{5,4},{6,7},{7,6},{8,9},{9,8},{10,11... | collective-permute-start | bytes 405512 | tf_op jit(solution)/shard_map/ppermute | solution.py:268
  322.3 26.8 %collective-permute-start.46 = (bf16[2,272,256]{2,1,0:T(8,128)(2,1)S(1)}, bf16[2,272,256]{2,1,0:T(8,128)(2,1)S(1)}, u32[]{:S(2)}, u32[]{:S(2)}) collective-permute-start(bf16[2,272,256]{2,1,0:T(8,128)(2,1)S(1)} %copy-done.87), channel_id=1, source_target_pairs={{0,8},{4,12},{8,0},{12,4},{1,9},{5,13},{9,1},{13,5},{2,10},{6,14},... | collective-permute-start | bytes 835592 | tf_op jit(solution)/shard_map/ppermute | solution.py:273
  328.7 20.3 %collective-permute-start.47 = (bf16[2,272,256]{2,1,0:T(8,128)(2,1)S(1)}, bf16[2,272,256]{2,1,0:T(8,128)(2,1)S(1)}, u32[]{:S(2)}, u32[]{:S(2)}) collective-permute-start(bf16[2,272,256]{2,1,0:T(8,128)(2,1)S(1)} %copy-done.85), channel_id=1, source_target_pairs={{0,4},{4,8},{8,12},{12,0},{1,5},{5,9},{9,13},{13,1},{2,6},{6,10},{... | collective-permute-start | bytes 835592 | tf_op jit(solution)/shard_map/ppermute | solution.py:273
  331.6 17.4 %collective-permute-start.48 = (bf16[2,272,256]{2,1,0:T(8,128)(2,1)S(1)}, bf16[2,272,256]{2,1,0:T(8,128)(2,1)S(1)}, u32[]{:S(2)}, u32[]{:S(2)}) collective-permute-start(bf16[2,272,256]{2,1,0:T(8,128)(2,1)S(1)} %get-tuple-element.209), channel_id=1, source_target_pairs={{0,12},{4,0},{8,4},{12,8},{1,13},{5,1},{9,5},{13,9},{2,14},{6,2},{... | collective-permute-start | bytes 835592 | tf_op jit(solution)/shard_map/ppermute | solution.py:273
  349.7 6.0 %collective-permute-start.53 = (bf16[272,256]{1,0:T(8,128)(2,1)S(1)}, bf16[272,256]{1,0:T(8,128)(2,1)S(1)}, u32[]{:S(2)}, u32[]{:S(2)}) collective-permute-start(bf16[272,256]{1,0:T(8,128)(2,1)S(1)} %get-tuple-element.216), channel_id=1, source_target_pairs={{0,1},{1,0},{2,3},{3,2},{4,5},{5,4},{6,7},{7,6},{8,9},{9,8},{10,11... | collective-permute-start | bytes 417800 | tf_op jit(solution)/shard_map/ppermute | solution.py:268
  350.2 10.5 %collective-permute-start.38 = (bf16[256,1024]{1,0:T(8,128)(2,1)S(1)}, bf16[256,1024]{1,0:T(8,128)(2,1)S(1)}, u32[]{:S(2)}, u32[]{:S(2)}) collective-permute-start(bf16[256,1024]{1,0:T(8,128)(2,1)S(1)} %pad_maximum_fusion.3), channel_id=1, source_target_pairs={{0,0},{2,16},{16,2},{18,18},{1,1},{3,17},{17,3},{19,19},{4,4},{6,2... | collective-permute-start | bytes 1572872 | tf_op jit(solution)/shard_map/ppermute | solution.py:1054
  353.0 13.3 %collective-permute-start.44 = (bf16[256,1024]{1,0:T(8,128)(2,1)S(1)}, bf16[256,1024]{1,0:T(8,128)(2,1)S(1)}, u32[]{:S(2)}, u32[]{:S(2)}) collective-permute-start(bf16[256,1024]{1,0:T(8,128)(2,1)S(1)} %add_convert_fusion.2), channel_id=1, source_target_pairs={{0,0},{2,16},{16,2},{18,18},{1,1},{3,17},{17,3},{19,19},{4,4},{6,2... | collective-permute-start | bytes 1572872 | tf_op jit(solution)/shard_map/ppermute | solution.py:1008
  355.8 11.6 %collective-permute-start.54 = (bf16[2,272,256]{2,1,0:T(8,128)(2,1)S(1)}, bf16[2,272,256]{2,1,0:T(8,128)(2,1)S(1)}, u32[]{:S(2)}, u32[]{:S(2)}) collective-permute-start(bf16[2,272,256]{2,1,0:T(8,128)(2,1)S(1)} %pad_maximum_fusion.4), channel_id=1, source_target_pairs={{0,16},{16,0},{1,17},{17,1},{2,18},{18,2},{3,19},{19,3},{4,20},{20... | collective-permute-start | bytes 835592 | tf_op jit(solution)/shard_map/ppermute | solution.py:268
  (112 other events, 603.4 us)
Sparse Core Ops, SparseCore 0:
  28.6 43.6 all-gather.4
  110.7 53.2 all-gather.6
  239.7 26.1 reduce-scatter.2
  278.7 24.9 reduce-scatter.4
